TPU v7x, 32 devices: a whole 2x2x4 slice. The times are simulated.
32 devices in a mesh: pipe: 8 (over y, x, core), seq: 4 (over z).
Axes of the slice: x: 2, y: 2, z: 4, core: 2. Of those that a mesh axis runs over, the one named last changes fastest.
Arguments:
- activations: bfloat16 [512, 4096], P('seq', 'pipe'), may hold values from -6 to 6
- norm_gain: bfloat16 [4096], P('pipe'), may hold values from 0.5 to 2
- w_qkv: bfloat16 [8, 4096, 384], P('pipe', 'seq'), may hold values from -1 to 1
- w_out: bfloat16 [8, 128, 4096], P('pipe', None, 'seq'), may hold values from -0.375 to 0.375
- block_mask: int32 [4, 4], replicated, may hold values from 0 to 1, as said below
- cotangent: bfloat16 [512, 4096], P('seq', 'pipe'), may hold values from -6 to 6
Outputs:
- output: bfloat16 [512, 4096], P('seq', 'pipe')
- input_grad: bfloat16 [512, 4096], P('seq', 'pipe')
Inputs may be any that keep to these rules, and one draw needn't show every extreme that they name: `block_mask`: every diagonal entry is 1; the rows hold uneven numbers of ones.
All inputs are finite; a program needn't handle non-finite values.
Results may differ from a plain program's by a relative error of at most 0.02.
The roundings to bfloat16 on the way count: a program that leaves them out, or rounds other values in their place, can miss the bound.
Values may be sent and summed in bfloat16 or wider, within the bound.
No kernel may reach another device: no remote copies, remote signals or barrier semaphores. Data moves between devices by JAX's collectives and lax.ppermute only.
A program may use at most 64 MiB of HBM per device.

v0:
```python
import math

import jax
import jax.numpy as jnp
from jax import lax
from jax.sharding import PartitionSpec as P

BLOCK = 128


def per_device(activations, norm_gain, w_qkv, w_out, block_mask, cotangent):
    complete_row_block, full_grad, full_gain = (
        lax.all_gather(activations, "pipe", axis=1, tiled=True),
        lax.all_gather(cotangent, "pipe", axis=1, tiled=True),
        lax.all_gather(norm_gain, "pipe", axis=0, tiled=True),
    )
    w_all, wo_all = (
        lax.all_gather(w_qkv, "seq", axis=1, tiled=True),
        lax.all_gather(w_out, "seq", axis=2, tiled=True),
    )
    w_head = w_all[0]
    wo_head = wo_all[0]
    head_dim = wo_head.shape[0]
    factor = 1.0 / math.sqrt(head_dim)
    rows = activations.shape[0]
    blocks_dev = rows // BLOCK
    place = lax.axis_index("seq")
    input_rows = complete_row_block.astype(jnp.float32)
    square_root_norm = lax.rsqrt(jnp.mean(input_rows * input_rows, axis=-1, keepdims=True) + 1e-05)
    gain = full_gain.astype(jnp.float32)
    normed = (input_rows * square_root_norm * gain).astype(jnp.bfloat16)
    normalized_input = input_rows * square_root_norm
    projected = jnp.dot(normed, w_head, preferred_element_type=jnp.float32)
    query = projected[:, :head_dim].astype(jnp.bfloat16)
    key_value = projected[:, head_dim:].astype(jnp.bfloat16)
    kv_all = lax.all_gather(key_value, "seq", axis=0, tiled=True)
    key_all = kv_all[:, :head_dim]
    value_all = kv_all[:, head_dim:]
    total_blocks = kv_all.shape[0] // BLOCK
    mask_rows = lax.dynamic_slice_in_dim(block_mask, place * blocks_dev, blocks_dev, 0)
    allowed = jnp.broadcast_to(
        mask_rows[:, None, :, None] > 0, (blocks_dev, BLOCK, total_blocks, BLOCK)
    )
    allowed = allowed.reshape(rows, kv_all.shape[0])
    scores = jnp.einsum("re,te->rt", query, key_all, preferred_element_type=jnp.float32) * factor
    scores = jnp.where(allowed, scores, -1e30)
    top = jnp.max(scores, axis=-1, keepdims=True)
    expd = jnp.where(allowed, jnp.exp(scores - top), 0.0)
    total = jnp.sum(expd, axis=-1, keepdims=True)
    probs = expd / total
    probs_round = probs.astype(jnp.bfloat16)
    attended = jnp.dot(probs_round, value_all, preferred_element_type=jnp.float32).astype(
        jnp.bfloat16
    )
    term = jnp.dot(attended, wo_head, preferred_element_type=jnp.float32)
    head_total = lax.psum_scatter(
        term.astype(jnp.bfloat16), "pipe", scatter_dimension=1, tiled=True
    ).astype(jnp.float32)
    output = (activations.astype(jnp.float32) + head_total).astype(jnp.bfloat16)
    d_att = jnp.einsum("rd,ed->re", full_grad, wo_head, preferred_element_type=jnp.float32).astype(
        jnp.bfloat16
    )
    d_probs = jnp.einsum("re,te->rt", d_att, value_all, preferred_element_type=jnp.float32)
    delta = jnp.sum(probs * d_probs, axis=-1, keepdims=True)
    d_scores = (probs * (d_probs - delta) * factor).astype(jnp.bfloat16)
    d_query = jnp.dot(d_scores, key_all, preferred_element_type=jnp.float32).astype(jnp.bfloat16)
    query_grad = jnp.concatenate([query, d_att], axis=1)
    log_total = top[:, 0] + jnp.log(total[:, 0])
    statistics = jnp.stack([log_total, delta[:, 0]], axis=0)
    query_all = lax.all_gather(query_grad, "seq", axis=0, tiled=True)
    stats_all = lax.all_gather(statistics, "seq", axis=1, tiled=True)
    queries_all = query_all[:, :head_dim]
    d_att_all = query_all[:, head_dim:]
    key_own = key_value[:, :head_dim]
    value_own = key_value[:, head_dim:]
    mask_cols = lax.dynamic_slice_in_dim(block_mask, place * blocks_dev, blocks_dev, 1)
    allowed_cols = jnp.broadcast_to(
        mask_cols[:, None, :, None] > 0, (total_blocks, BLOCK, blocks_dev, BLOCK)
    )
    allowed_cols = allowed_cols.reshape(kv_all.shape[0], rows)
    scores_cols = (
        jnp.einsum("te,re->tr", queries_all, key_own, preferred_element_type=jnp.float32) * factor
    )
    probs_cols = jnp.where(
        allowed_cols,
        jnp.exp(jnp.where(allowed_cols, scores_cols, -1e30) - stats_all[0][:, None]),
        0.0,
    )
    d_value_own = jnp.einsum(
        "tr,te->re", probs_cols.astype(jnp.bfloat16), d_att_all, preferred_element_type=jnp.float32
    )
    d_probs_cols = jnp.einsum("te,re->tr", d_att_all, value_own, preferred_element_type=jnp.float32)
    score_column_gradients = (probs_cols * (d_probs_cols - stats_all[1][:, None]) * factor).astype(
        jnp.bfloat16
    )
    d_key_own = jnp.einsum(
        "tr,te->re", score_column_gradients, queries_all, preferred_element_type=jnp.float32
    )
    local_gradients = jnp.concatenate(
        [d_key_own.astype(jnp.bfloat16), d_value_own.astype(jnp.bfloat16)], axis=1
    )
    d_proj = jnp.concatenate([d_query, local_gradients], axis=1)
    d_normed = jnp.einsum("rc,dc->rd", d_proj, w_head, preferred_element_type=jnp.float32)
    rescaled_values = d_normed * gain
    gradient_component = square_root_norm * (
        rescaled_values
        - normalized_input * jnp.mean(rescaled_values * normalized_input, axis=-1, keepdims=True)
    )
    grad_total = lax.psum_scatter(
        gradient_component.astype(jnp.bfloat16), "pipe", scatter_dimension=1, tiled=True
    ).astype(jnp.float32)
    input_grad = (cotangent.astype(jnp.float32) + grad_total).astype(jnp.bfloat16)
    return (output, input_grad)


def solution(mesh):
    in_specs = (
        P("seq", "pipe"),
        P("pipe"),
        P("pipe", "seq", None),
        P("pipe", None, "seq"),
        P(),
        P("seq", "pipe"),
    )
    out_specs = (P("seq", "pipe"), P("seq", "pipe"))
    return jax.shard_map(
        per_device, mesh=mesh, in_specs=in_specs, out_specs=out_specs, check_vma=False
    )
```

profile of v0, /device:TPU:24, one launch (start us, length us, event | category | flops | bytes accessed | tf_op | source)
XLA Modules:
  0.0 255.3 jit_solution(180428671076649715)
XLA Ops:
  7.2 0.7 all-gather.6.cloned.1.call-update
  7.9 0.7 all-gather.10.cloned.1.call-update
  8.7 0.7 all-gather.12.cloned.1.call-update
  10.0 0.7 reshape.64
  10.7 8.9 %all-gather = bf16[8,1,512]{2,1,0:T(2,128)(2,1)S(1)} all-gather(bf16[1,1,512]{2,1,0:T(2,128)(2,1)S(1)} %reshape.64), channel_id=1, replica_groups=mesh['pipe'=8,'seq'=4] {'pipe'}, dimensions={0}, use_global_device_ids=true | all-gather | bytes 9216 | tf_op jit(solution)/shard_map/all_gather | solution.py:15
  19.6 0.9 fusion.58
  20.5 0.7 compare_bitcast_fusion
  21.3 13.1 %all-gather.6.cloned.1.call-done = bf16[128,4096]{1,0:T(8,128)(2,1)} async-done(((bf16[128,512]{1,0:T(8,128)(2,1)}), bf16[128,4096]{1,0:T(8,128)(2,1)}) %all-gather.6.cloned.1.call-update) | async-done | bytes 1048592 | tf_op jit(solution)/shard_map/all_gather | solution.py:13
  34.5 1.6 fusion.11
  36.1 26.5 %all-gather.10.cloned.1.call-done = bf16[1,128,4096]{2,1,0:T(8,128)(2,1)} async-done(((bf16[1,128,1024]{2,1,0:T(8,128)(2,1)}), bf16[1,128,4096]{2,1,0:T(8,128)(2,1)}) %all-gather.10.cloned.1.call-update) | async-done | bytes 1048592 | tf_op jit(solution)/shard_map/all_gather | solution.py:19
  62.6 26.4 %all-gather.12.cloned.1.call-done = bf16[128,4096]{1,0:T(8,128)(2,1)} async-done(((bf16[128,512]{1,0:T(8,128)(2,1)}), bf16[128,4096]{1,0:T(8,128)(2,1)}) %all-gather.12.cloned.1.call-update) | async-done | bytes 1048592 | tf_op jit(solution)/shard_map/all_gather | solution.py:14
  89.0 2.0 convolution_convert_fusion.3
  91.0 60.4 %all-gather.8.cloned.1.call-done = bf16[1,4096,384]{2,1,0:T(8,128)(2,1)} async-done(((bf16[1,1024,384]{2,1,0:T(8,128)(2,1)}), bf16[1,4096,384]{2,1,0:T(8,128)(2,1)}) %all-gather.8.cloned.1.call-update) | async-done | bytes 3145744 | tf_op jit(solution)/shard_map/all_gather | solution.py:18
  151.3 2.7 %fusion.20 = bf16[128,384]{1,0:T(8,128)(2,1)S(1)} fusion(bf16[1,4096,384]{2,1,0:T(8,128)(2,1)} %all-gather.8.cloned.1.call-done, bf16[128,4096]{1,0:T(8,128)(2,1)S(1)} %copy-done, f32[4096]{0:T(1024)S(1)} %bitcast.28, f32[128]{0:T(128)S(1)} %add_rsqrt_fusion), kind=kOutput, calls=%fused_computation.27 | convolution fusion | flops 404799488 | bytes 4309504 | tf_op jit(solution)/shard_map/dot_general | solution.py:33
  154.1 14.1 %all_gather.27 = bf16[512,256]{1,0:T(8,128)(2,1)S(1)} all-gather(bf16[128,256]{1,0:T(8,128)(2,1)S(1)} %slice.45), channel_id=1, replica_groups=mesh['pipe'=8,'seq'=4] {'seq'}, dimensions={0}, use_global_device_ids=true | all-gather | bytes 327680 | tf_op jit(solution)/shard_map/all_gather | solution.py:36
  168.7 1.6 convolution_convert_fusion
  170.7 9.2 %all_gather.31 = f32[2,512]{1,0:T(2,128)S(1)} all-gather(f32[2,128]{1,0:T(2,128)S(1)} %pad_maximum_fusion.1), channel_id=1, replica_groups=mesh['pipe'=8,'seq'=4] {'seq'}, dimensions={1}, use_global_device_ids=true | all-gather | bytes 5120 | tf_op jit(solution)/shard_map/all_gather | solution.py:71
  179.9 13.9 %all_gather.30 = bf16[512,256]{1,0:T(8,128)(2,1)S(1)} all-gather(bf16[128,256]{1,0:T(8,128)(2,1)S(1)} %pad_maximum_fusion), channel_id=1, replica_groups=mesh['pipe'=8,'seq'=4] {'seq'}, dimensions={0}, use_global_device_ids=true | all-gather | bytes 327680 | tf_op jit(solution)/shard_map/all_gather | solution.py:70
  195.0 3.1 %fusion.7 = (f32[128]{0:T(128)S(1)}, f32[128,4096]{1,0:T(8,128)S(1)}) fusion(bf16[128,4096]{1,0:T(8,128)(2,1)S(1)} %copy-done, f32[128]{0:T(128)S(1)} %add_rsqrt_fusion, f32[4096]{0:T(1024)S(1)} %bitcast.29, bf16[1,4096,384]{2,1,0:T(8,128)(2,1)} %all-gather.8.cloned.1.call-done, bf16[128,128]{1,0:T(8,128)(2,1)S(1)} %convolution_convert_fusion.1, ...), kind=kOutput, calls=%fused_computation.11 | convolution fusion | flops 405569408 | bytes 6407168 | tf_op jit(solution)/shard_map/rc,dc->rd/dot_general | solution.py:103
  198.1 1.5 fusion.10
  199.7 8.2 %reduce-scatter.3.cloned.1.call-done = bf16[128,512]{1,0:T(8,128)(2,1)} async-done(((bf16[128,4096]{1,0:T(8,128)(2,1)}), bf16[128,512]{1,0:T(8,128)(2,1)}) %reduce-scatter.3.cloned.1.call-update) | async-done | bytes 131088 | tf_op jit(solution)/shard_map/reduce_scatter | solution.py:56
  207.8 1.6 add_convert_fusion.1
  209.4 37.5 %reduce-scatter.5.cloned.1.call-done = bf16[128,512]{1,0:T(8,128)(2,1)} async-done(((bf16[128,4096]{1,0:T(8,128)(2,1)}), bf16[128,512]{1,0:T(8,128)(2,1)}) %reduce-scatter.5.cloned.1.call-update) | async-done | bytes 131088 | tf_op jit(solution)/shard_map/reduce_scatter | solution.py:109
  246.9 1.6 add_convert_fusion
  (35 shorter events, 2.9 us)
Async XLA Ops:
  7.2 27.3 %all-gather.6.cloned.1.call-start = ((), (), s32[]{:S(2)}) async-start(), calls=%async_computation.2 | async-start | bytes 1179648 | tf_op jit(solution)/shard_map/all_gather | solution.py:13
  7.9 54.7 %all-gather.10.cloned.1.call-start = ((), (), s32[]{:S(2)}) async-start(), calls=%async_computation.4 | async-start | bytes 1310720 | tf_op jit(solution)/shard_map/all_gather | solution.py:19
  8.6 80.3 %all-gather.12.cloned.1.call-start = ((), (), s32[]{:S(2)}) async-start(), calls=%async_computation.6 | async-start | bytes 1179648 | tf_op jit(solution)/shard_map/all_gather | solution.py:14
  9.4 141.9 %all-gather.8.cloned.1.call-start = ((), (), s32[]{:S(2)}) async-start(), calls=%async_computation.3 | async-start | bytes 3932160 | tf_op jit(solution)/shard_map/all_gather | solution.py:18
  10.0 197.8 %reduce-scatter.3.cloned.1.call-start = ((), (), s32[]{:S(2)}) async-start(), calls=%async_computation.5 | async-start | bytes 1179648 | tf_op jit(solution)/shard_map/reduce_scatter | solution.py:56
  34.5 116.9 %copy-start = (bf16[128,4096]{1,0:T(8,128)(2,1)S(1)}, bf16[128,4096]{1,0:T(8,128)(2,1)}, u32[]{:S(2)}) copy-start(bf16[128,4096]{1,0:T(8,128)(2,1)} %all-gather.6.cloned.1.call-done) | copy-start | bytes 3145732
  151.3 17.4 %copy-start.1 = (bf16[1,128,4096]{2,1,0:T(8,128)(2,1)S(1)}, bf16[1,128,4096]{2,1,0:T(8,128)(2,1)}, u32[]{:S(2)}) copy-start(bf16[1,128,4096]{2,1,0:T(8,128)(2,1)} %all-gather.10.cloned.1.call-done) | copy-start | bytes 3145732
  170.3 76.6 %reduce-scatter.5.cloned.1.call-start = ((), (), s32[]{:S(2)}) async-start(), calls=%async_computation.7 | async-start | bytes 1179648 | tf_op jit(solution)/shard_map/reduce_scatter | solution.py:109
  198.1 9.7 %copy-start.2 = (bf16[128,512]{1,0:T(8,128)(2,1)S(1)}, bf16[128,512]{1,0:T(8,128)(2,1)}, u32[]{:S(2)}) copy-start(bf16[128,512]{1,0:T(8,128)(2,1)} %param.6) | copy-start | bytes 393220
  198.1 48.8 %copy-start.3 = (bf16[128,512]{1,0:T(8,128)(2,1)S(1)}, bf16[128,512]{1,0:T(8,128)(2,1)}, u32[]{:S(2)}) copy-start(bf16[128,512]{1,0:T(8,128)(2,1)} %param.11) | copy-start | bytes 393220
Sparse Core Ops, SparseCore 0:
  9.9 24.5 all-gather.5
  36.0 26.4 all-gather.9
  64.5 24.4 all-gather.11
  90.4 60.8 all-gather.7
  170.4 37.3 reduce-scatter.2
  210.8 36.0 reduce-scatter.4
where the time goes:
time: 257 us; the launch traced here: 255 us
  waiting for transfers between devices  175 us (68%)
  blocking collectives  46.1 us (18%)
  between operations  14.2 us (6%)
  matrix products  11.1 us (4%)
  other arithmetic  8.1 us (3%)
    all_gather x1, waiting for transfers between devices, per_device(): lax.all_gather(w_qkv, 'seq', axis=1, tiled=True)  60.4 us
    reduce_scatter x1, waiting for transfers between devices, per_device(): lax.psum_scatter(gradient_component.astype(jnp.bfloat16), 'pipe', scatter...  37.5 us
    all_gather x1, waiting for transfers between devices, per_device(): lax.all_gather(w_out, 'seq', axis=2, tiled=True)  26.5 us
    all_gather x1, waiting for transfers between devices, per_device(): lax.all_gather(cotangent, 'pipe', axis=1, tiled=True)  26.4 us
    all_gather x1, blocking collectives, per_device(): kv_all = lax.all_gather(key_value, 'seq', axis=0, tiled=True)  14.1 us
    all_gather x1, blocking collectives, per_device(): query_all = lax.all_gather(query_grad, 'seq', axis=0, tiled=True)  13.9 us
    all_gather x1, waiting for transfers between devices, per_device(): lax.all_gather(activations, 'pipe', axis=1, tiled=True)  13.1 us
    all_gather x1, blocking collectives, per_device(): stats_all = lax.all_gather(statistics, 'seq', axis=1, tiled=True)  9.25 us
  transfers between devices with their start and end apart: 6, of which 6 were waited for; matrix products, arithmetic and copies ran while one was open for 5% of the time, Pallas kernels for 0%

commit v1 on v0

v1 whole, which is shorter than its diff:
```python
import functools
import math

import jax
import jax.numpy as jnp
from jax import lax
from jax.experimental import pallas as pl
from jax.experimental.pallas import tpu as pltpu
from jax.sharding import PartitionSpec as P

EPS = 1e-05
VMEM_LIMIT = 48 * 1024 * 1024
STAT = 128
AXES = ("pipe", "seq")
F32 = jnp.float32
BF16 = jnp.bfloat16


def place():
    pipe = lax.axis_index("pipe")
    return pipe // 2, pipe % 2, lax.axis_index("seq")


def nt(a, b):
    return lax.dot_general(a, b, (((1,), (1,)), ((), ())), preferred_element_type=F32)


def tn(a, b):
    return lax.dot_general(a, b, (((0,), (0,)), ((), ())), preferred_element_type=F32)


def nn(a, b):
    return jnp.dot(a, b, preferred_element_type=F32)


def span(index, size):
    if isinstance(index, int):
        return pl.ds(index * size, size)
    return pl.ds(pl.multiple_of(index * size, size), size)


def call(kernel, out_shape, *args, scratch=(), smem=()):
    specs = [
        pl.BlockSpec(memory_space=pltpu.SMEM if i in smem else pltpu.VMEM) for i in range(len(args))
    ]
    return pl.pallas_call(
        kernel,
        out_shape=out_shape,
        in_specs=specs,
        out_specs=jax.tree.map(lambda _: pl.BlockSpec(memory_space=pltpu.VMEM), out_shape),
        scratch_shapes=list(scratch),
        compiler_params=pltpu.CompilerParams(vmem_limit_bytes=VMEM_LIMIT),
    )(*args)


def shape(*dims, dtype=BF16):
    return jax.ShapeDtypeStruct(dims, dtype)


def each(n, body):
    if n <= 4:
        for e in range(n):
            body(e)
    else:
        lax.fori_loop(0, n, lambda e, carry: (body(e), carry)[1], 0)


def stack_kernel(own, sib, out):
    _, core, _ = place()
    rows, feats = own.shape[0], out.shape[1]
    out[:rows, :] = own[:, span(core, feats)]
    out[rows:, :] = sib[:, span(core, feats)]


def rows_kernel(x, gain, out):
    rows, feats = x.shape
    out[:rows, :] = x[...]
    out[rows:, :] = jnp.broadcast_to(gain[...], (16, feats))


def project_kernel(n, w, *refs):
    same, sib, outs = refs[:n], refs[n : 2 * n], refs[2 * n : 3 * n]
    own_squares, high, low, held, held_squares = refs[3 * n :]
    chip, core, plane = place()
    feats = same[0].shape[1]
    rows = same[0].shape[0] - 16
    width = w.shape[1]
    ones = jnp.ones((8, feats), BF16)
    line = lax.broadcasted_iota(jnp.int32, (16, rows), 0)

    def parts(value):
        first = value.astype(BF16)
        return first, (value - first.astype(F32)).astype(BF16)

    total = jnp.zeros((n * rows, width), F32)
    def gain_of(blocks):
        chosen = jnp.zeros((8, feats), F32)
        for d in range(n):
            lines = blocks[d][rows:, :].astype(F32)[:8]
            chosen += jnp.where(jnp.bitwise_xor(chip, d) == plane, lines, 0.0)
        return chosen[0:1, :]

    gains = gain_of(same), gain_of(sib)
    for d in range(n):
        slot = jnp.bitwise_xor(chip, d)
        squares = jnp.zeros((8, rows), F32)
        for i, blocks in enumerate((same, sib)):
            values = blocks[d][:rows, :].astype(F32)
            at = (span(slot, rows), slice(i * feats, (i + 1) * feats))
            high[at], low[at] = parts(values * gains[i])
            square_high, square_low = parts(values * values)
            squares += nt(ones, square_high) + nt(ones, square_low)
        held_squares[slot] = squares
    w_same, w_sib = w[span(core, feats), :], w[span(1 - core, feats), :]
    product = nn(high[:, :feats], w_same) + nn(low[:, :feats], w_same)
    product += nn(high[:, feats:], w_sib) + nn(low[:, feats:], w_sib)
    held[...] = product
    outs[0][...] = held[:rows, :]
    own_squares[...] = held_squares[0]
    for e in range(1, n):
        outs[e][:rows, :] = held[e * rows : (e + 1) * rows, :].astype(BF16)
        squares = held_squares[e][0:1, :]
        first = squares.astype(BF16).astype(F32)
        stat = jnp.where(line == 0, first, jnp.where(line == 1, squares - first, 0.0))
        outs[e][rows:, :] = jnp.zeros((16, width), BF16)
        outs[e][rows:, :rows] = stat.astype(BF16)


def combine_kernel(n, features, squares, d_att, d_att_sib, *refs):
    parts, (out, root) = refs[:n], refs[n:]
    rows, width = parts[0].shape
    total = parts[0][...]
    sums = squares[0:1, :]
    for part in parts[1:]:
        total += part[:rows, :].astype(F32)
        sums += jnp.sum(part[rows:, :rows].astype(F32), axis=0, keepdims=True)
    scale = jnp.broadcast_to(lax.rsqrt(sums / features + EPS), (rows, rows)).T
    root[...] = scale
    out[:, :width] = (total * scale[:, :1]).astype(BF16)
    out[:, width:] = (d_att[...] + d_att_sib[...]).astype(BF16)


def cotangent_kernel(n, *refs):
    cots, weights, (own, sib, held) = refs[:n], refs[n : 2 * n], refs[2 * n :]
    chip, _, plane = place()
    turn = jnp.bitwise_xor(chip, plane)
    rows, head = own.shape
    for d in range(n):
        held[jnp.bitwise_xor(turn, d)] = cots[d][...]
    total = jnp.zeros((rows, 2 * head), F32)
    for e in range(n):
        total += nt(held[e], weights[e][...])
    own[...] = total[:, :head]
    sib[...] = total[:, head:]


def split_stat(column):
    high = column.astype(BF16).astype(F32)
    lane = lax.broadcasted_iota(jnp.int32, (column.shape[0], STAT), 1)
    return jnp.where(lane == 0, high, jnp.where(lane == 1, column - high, 0.0)).astype(BF16)


def attention_kernel(n, features, mask, *refs):
    blocks = refs[:n]
    attended_out, d_proj, held, probs_held, d_scores_held = refs[n:]
    _, _, plane = place()
    rows = blocks[0].shape[0]
    head = blocks[0].shape[1] // 4
    factor = 1.0 / math.sqrt(head)
    for e in range(n):
        held[e * rows : (e + 1) * rows, :] = blocks[e][...]
    key = held[:, head : 2 * head]
    value = held[:, 2 * head : 3 * head]
    column_block = lax.broadcasted_iota(jnp.int32, (1, n * rows), 1) // rows

    def one_block(e):
        at = span(e, rows)
        row_plane = jnp.bitwise_xor(plane, e)
        allowed = jnp.zeros((1, n * rows), jnp.int32)
        for other in range(n):
            entry = mask[row_plane, jnp.bitwise_xor(plane, other)]
            allowed = jnp.where(column_block == other, entry, allowed)
        scores = jnp.where(allowed > 0, nt(held[at, :head], key) * factor, -1e30)
        expd = jnp.exp(scores - jnp.max(scores, axis=-1, keepdims=True))
        probs = expd / jnp.sum(expd, axis=-1, keepdims=True)
        probs_round = probs.astype(BF16)
        d_probs = nt(held[at, 3 * head :], value)
        delta = jnp.sum(probs * d_probs, axis=-1, keepdims=True)
        d_scores = (probs * (d_probs - delta) * factor).astype(BF16)
        d_proj[at, :head] = nn(d_scores, key).astype(BF16)
        probs_held[at, :] = probs_round
        d_scores_held[at, :] = d_scores

    each(n, one_block)
    d_proj[:, head : 2 * head] = tn(d_scores_held[...], held[:, :head]).astype(BF16)
    d_proj[:, 2 * head :] = tn(probs_held[...], held[:, 3 * head :]).astype(BF16)
    attended_out[:, :head] = nn(probs_held[:rows, :], value).astype(BF16)
    products = d_proj[:rows, :].astype(F32) * held[:rows, : 3 * head].astype(F32)
    mean = jnp.sum(products, axis=1, keepdims=True) / features
    attended_out[:, head:] = split_stat(mean)


def back_own_kernel(d_proj, w, out):
    _, core, _ = place()
    out[...] = nt(d_proj[...], w[span(core, out.shape[1]), :])


def back_sum_kernel(n, own, d_proj, w, *refs):
    outs, held = refs[:n], refs[n]
    chip, core, _ = place()
    rows, feats = outs[0].shape
    held[...] = (own[...] + nt(d_proj[...], w[span(core, feats), :])).astype(BF16)
    for d in range(n):
        outs[d][...] = held[span(jnp.bitwise_xor(chip, d), rows), :]


def term_kernel(n, own, sib, *refs):
    weights, outs, held = refs[:n], refs[n : 2 * n], refs[2 * n]
    chip, _, plane = place()
    turn = jnp.bitwise_xor(chip, plane)
    head = weights[0].shape[0] // 2
    feats = weights[0].shape[1]
    for e in range(n):
        term = nn(own[:, :head], weights[e][:head, :]) + nn(sib[:, :head], weights[e][head:, :])
        held[jnp.bitwise_xor(turn, e)] = term.astype(BF16)
    means = own[:, head:].astype(F32) + sib[:, head:].astype(F32)
    stat = split_stat(jnp.sum(means, axis=1, keepdims=True))
    for d in range(n):
        outs[d][:, :feats] = held[d]
        outs[d][:, feats:] = stat


def sum_kernel(n, *refs):
    total = refs[0][...].astype(F32)
    for part in refs[1:n]:
        total += part[...].astype(F32)
    refs[n][...] = total.astype(BF16)


def finish_output_kernel(n, x, *refs):
    parts, (out, mean) = refs[:n], refs[n:]
    feats = x.shape[1]
    total = parts[0][...].astype(F32)
    for part in parts[1:]:
        total += part[...].astype(F32)
    out[...] = (x[...].astype(F32) + total[:, :feats]).astype(BF16)
    mean[...] = jnp.broadcast_to(jnp.sum(total[:, feats:], axis=1, keepdims=True), mean.shape)


def finish_grad_kernel(x, gain, cot, root, mean, grad, out):
    scale = root[:, :1]
    shift = scale * mean[:, :1]
    centred = grad[...].astype(F32) * gain[...].astype(F32) - x[...].astype(F32) * shift
    out[...] = (cot[...].astype(F32) + scale * centred).astype(BF16)


def per_device(n, activations, norm_gain, w_qkv, w_out, block_mask, cotangent):
    rows, feats = activations.shape
    features = feats * 2 * n
    head = w_out.shape[1]
    width = w_qkv.shape[2]
    tokens = n * rows

    def move(value, target):
        pairs = []
        for chip in range(n):
            for core in range(2):
                for plane in range(n):
                    to_chip, to_core, to_plane = target(chip, core, plane)
                    pairs.append(((2 * chip + core) * n + plane, (2 * to_chip + to_core) * n + to_plane))
        return lax.ppermute(value, AXES, pairs)

    def swap(value):
        return move(value, lambda c, k, z: (c, 1 - k, z))

    def to_chip(value, d):
        return move(value, lambda c, k, z: (c ^ d, k, z))

    def to_plane(value, e):
        return move(value, lambda c, k, z: (c, k, z ^ e))

    def after(value, *earlier):
        return lax.optimization_barrier((value, *earlier))[0]

    w = w_qkv[0]
    wo = w_out[0]

    x_held = move(activations, lambda c, k, z: (z ^ c, k, c))
    gain = norm_gain.reshape(1, feats)
    wo_sib = swap(wo)
    cots = [cotangent] + [to_chip(cotangent, d) for d in range(1, n)]
    own = call(stack_kernel, shape(2 * head, feats), wo, wo_sib)
    order, step = [0, n // 2], n // 2
    far = to_plane(own, step)
    x_held, *cots = lax.optimization_barrier((x_held, *cots))
    x_held = call(rows_kernel, shape(rows + 16, feats), x_held, gain)
    x_same, x_sib = [x_held], [swap(x_held)]
    for d in range(1, n):
        block = to_chip(x_held, d)
        if d == min(3, n - 1):
            block, far = lax.optimization_barrier((block, far))
        x_same.append(block)
        x_sib.append(swap(block))
    weights = [own, far]
    while step > 1:
        step //= 2
        ready = [after(part, x_sib[0 if i == 0 else 0]) for i, part in enumerate(weights)]
        weights += [to_plane(part, step) for part in ready]
        order += [o ^ step for o in order]
    *parts, own_squares = call(
        functools.partial(project_kernel, n),
        [shape(rows, width, dtype=F32)]
        + [shape(rows + 16, width)] * (n - 1)
        + [shape(8, rows, dtype=F32)],
        w, *x_same, *x_sib,
        scratch=[
            pltpu.VMEM((n * rows, 2 * feats), BF16),
            pltpu.VMEM((n * rows, 2 * feats), BF16),
            pltpu.VMEM((n * rows, width), F32),
            pltpu.VMEM((n, 8, rows), F32),
        ],
    )
    parts = [parts[0]] + [to_plane(parts[e], e) for e in range(1, n)]

    weights = [weights[order.index(e)] for e in range(n)]
    d_att, d_att_sib = call(
        functools.partial(cotangent_kernel, n),
        [shape(rows, head, dtype=F32)] * 2,
        *cots, *weights,
        scratch=[pltpu.VMEM((n, rows, feats), BF16)],
    )
    d_att_sib = swap(d_att_sib)
    mixed, root = call(
        functools.partial(combine_kernel, n, features),
        (shape(rows, width + head), shape(rows, rows, dtype=F32)),
        own_squares, d_att, d_att_sib, *parts,
    )
    w_sib = swap(after(w, mixed))
    mixed = [mixed] + [to_plane(mixed, e) for e in range(1, n)]
    attended, d_proj = call(
        functools.partial(attention_kernel, n, features),
        (shape(rows, head + STAT), shape(tokens, width)),
        block_mask, *mixed,
        smem=(0,),
        scratch=[
            pltpu.VMEM((tokens, width + head), BF16),
            pltpu.VMEM((tokens, tokens), BF16),
            pltpu.VMEM((tokens, tokens), BF16),
        ],
    )
    d_proj_sib, attended_sib = lax.optimization_barrier((swap(d_proj), swap(attended)))
    back = call(back_own_kernel, shape(tokens, feats, dtype=F32), d_proj, w)
    grads = call(
        functools.partial(back_sum_kernel, n),
        [shape(rows, feats)] * n,
        back, d_proj_sib, w_sib,
        scratch=[pltpu.VMEM((tokens, feats), BF16)],
    )
    grads = [grads[0]] + [to_chip(grads[d], d) for d in range(1, n)]
    terms = call(
        functools.partial(term_kernel, n),
        [shape(rows, feats + STAT)] * n,
        attended, attended_sib, *weights,
        scratch=[pltpu.VMEM((n, rows, feats), BF16)],
    )
    terms = [terms[0]] + [to_chip(terms[d], d) for d in range(1, n)]
    grad = call(functools.partial(sum_kernel, n), shape(rows, feats), *grads)
    grad = move(grad, lambda c, k, z: (z, k, z ^ c))
    output, mean = call(
        functools.partial(finish_output_kernel, n),
        (shape(rows, feats), shape(rows, STAT, dtype=F32)),
        activations, *terms,
    )
    input_grad = call(
        finish_grad_kernel, shape(rows, feats),
        activations, gain, cotangent, root, mean, grad,
    )
    return (output, input_grad)


def solution(mesh):
    in_specs = (
        P("seq", "pipe"),
        P("pipe"),
        P("pipe", "seq", None),
        P("pipe", None, "seq"),
        P(),
        P("seq", "pipe"),
    )
    out_specs = (P("seq", "pipe"), P("seq", "pipe"))
    n = mesh.shape["seq"]
    assert mesh.shape["pipe"] == 2 * n
    return jax.shard_map(
        functools.partial(per_device, n),
        mesh=mesh,
        in_specs=in_specs,
        out_specs=out_specs,
        check_vma=False,
    )
```

time: 257 us -> 88.1 us (0.34)
  waiting for transfers between devices: 175 us -> 39.7 us
  blocking collectives: 46.1 us -> 0 us
  starting transfers between devices: 0.23 us -> 37.5 us
  between operations: 14.2 us -> 0.81 us
  matrix products: 11.1 us -> 0 us
  Pallas kernels: 0 us -> 8.72 us
  other arithmetic: 8.1 us -> 0 us
    all_gather x4 -> x0, waiting for transfers between devices: 126 us -> none  [the longest x1 60.4 us: per_device(): lax.all_gather(w_qkv, 'seq', axis=1, tiled=True)]
    all_gather x4 -> x0, blocking collectives: 46.1 us -> none  [the longest x1 14.1 us: per_device(): kv_all = lax.all_gather(key_value, 'seq', axis=0, tiled=True)]
    reduce_scatter x2 -> x0, waiting for transfers between devices: 45.7 us -> none  [the longest x1 37.5 us: per_device(): lax.psum_scatter(gradient_component.astype(jnp.bfloat16), 'pipe', scatter...]
    ppermute x0 -> x32, waiting for transfers between devices: none -> 39.7 us  [move(): return lax.ppermute(value, AXES, pairs)]
    ppermute x0 -> x32, starting transfers between devices: none -> 37.5 us  [move(): return lax.ppermute(value, AXES, pairs)]
    dot_general x10 -> x0, matrix products: 11.1 us -> none  [the longest x1 3.13 us: per_device(): jnp.einsum('rc,dc->rd', d_proj, w_head, preferred_element_type=jnp.float32)]
    pallas_call x0 -> x12, Pallas kernels: none -> 8.72 us  [call(): pl.pallas_call(kernel, out_shape=out_shape, in_specs=specs, out_specs=jax...]
    convert_element_type x4 -> x0, other arithmetic: 4.69 us -> none  [the longest x1 1.59 us: per_device(): output = (activations.astype(jnp.float32) + head_total).astype(jnp.bfloat16)]
  transfers between devices with their start and end apart: 6 -> 32, of which waited for: 6 -> 18; matrix products, arithmetic and copies ran while one was open for 5% -> 0% of each run, Pallas kernels for 0% -> 8%
where the time goes in v1:
time: 88.1 us; the launch traced here: 87.9 us
  waiting for transfers between devices  39.7 us (45%)
  starting transfers between devices  37.5 us (43%)
  Pallas kernels  8.72 us (10%)
  local copies, waits for them, and re-layouts  1.17 us (1%)
    ppermute x32, waiting for transfers between devices, move(): return lax.ppermute(value, AXES, pairs)  39.7 us
    ppermute x32, starting transfers between devices, move(): return lax.ppermute(value, AXES, pairs)  37.5 us
    pallas_call x12, Pallas kernels, call(): pl.pallas_call(kernel, out_shape=out_shape, in_specs=specs, out_specs=jax...  8.72 us
  transfers between devices with their start and end apart: 32, of which 18 were waited for; matrix products, arithmetic and copies ran while one was open for 0% of the time, Pallas kernels for 8%

profile of v1, /device:TPU:24, one launch (start us, length us, event | category | flops | bytes accessed | tf_op | source)
XLA Modules:
  0.0 87.9 jit_solution(16927151602458417843)
XLA Ops:
  0.7 4.1 %collective-permute-start = (bf16[128,512]{1,0:T(8,128)(2,1)}, bf16[128,512]{1,0:T(8,128)(2,1)S(1)}, u32[]{:S(2)}, u32[]{:S(2)}) collective-permute-start(bf16[128,512]{1,0:T(8,128)(2,1)} %x.3), channel_id=1, source_target_pairs={{0,0},{1,8},{2,16},{3,24},{4,4},{5,12},{6,20},{7,28},{8,9},{9,1},{... | collective-permute-start | bytes 393224 | tf_op jit(solution)/shard_map/ppermute | solution.py:271
  7.1 1.4 %collective-permute-start.1 = (bf16[128,512]{1,0:T(8,128)(2,1)}, bf16[128,512]{1,0:T(8,128)(2,1)S(1)}, u32[]{:S(2)}, u32[]{:S(2)}) collective-permute-start(bf16[128,512]{1,0:T(8,128)(2,1)} %cot.1), channel_id=1, source_target_pairs={{0,8},{1,9},{2,10},{3,11},{4,12},{5,13},{6,14},{7,15},{8,0},{9,1},... | collective-permute-start | bytes 393224 | tf_op jit(solution)/shard_map/ppermute | solution.py:271
  11.3 3.7 %collective-permute-done.3.refs_3_ = bf16[128,512]{1,0:T(8,128)(2,1)S(1)} collective-permute-done((bf16[128,512]{1,0:T(8,128)(2,1)}, bf16[128,512]{1,0:T(8,128)(2,1)S(1)}, u32[]{:S(2)}, u32[]{:S(2)}) %collective-permute-start.3) | collective-permute-done | bytes 131104 | tf_op jit(solution)/shard_map/ppermute | solution.py:271
  15.3 1.7 %collective-permute-start.6 = (bf16[144,512]{1,0:T(8,128)(2,1)S(1)}, bf16[144,512]{1,0:T(8,128)(2,1)S(1)}, u32[]{:S(2)}, u32[]{:S(2)}) collective-permute-start(bf16[144,512]{1,0:T(8,128)(2,1)S(1)} %shard_map.77.refs_0_), channel_id=1, source_target_pairs={{0,24},{1,25},{2,26},{3,27},{4,28},{5,29},{6,30},{7,31},{8,16},{9,... | collective-permute-start | bytes 442376 | tf_op jit(solution)/shard_map/ppermute | solution.py:271
  17.0 4.3 %collective-permute-start.5 = (bf16[144,512]{1,0:T(8,128)(2,1)S(1)}, bf16[144,512]{1,0:T(8,128)(2,1)S(1)}, u32[]{:S(2)}, u32[]{:S(2)}) collective-permute-start(bf16[144,512]{1,0:T(8,128)(2,1)S(1)} %shard_map.77.refs_0_), channel_id=1, source_target_pairs={{0,16},{1,17},{2,18},{3,19},{4,20},{5,21},{6,22},{7,23},{8,24},{9,... | collective-permute-start | bytes 442376 | tf_op jit(solution)/shard_map/ppermute | solution.py:271
  21.3 1.4 %collective-permute-start.4 = (bf16[144,512]{1,0:T(8,128)(2,1)S(1)}, bf16[144,512]{1,0:T(8,128)(2,1)S(1)}, u32[]{:S(2)}, u32[]{:S(2)}) collective-permute-start(bf16[144,512]{1,0:T(8,128)(2,1)S(1)} %shard_map.77.refs_0_), channel_id=1, source_target_pairs={{0,8},{1,9},{2,10},{3,11},{4,12},{5,13},{6,14},{7,15},{8,0},{9,1},... | collective-permute-start | bytes 442376 | tf_op jit(solution)/shard_map/ppermute | solution.py:271
  23.2 2.7 %collective-permute-start.14 = (bf16[256,512]{1,0:T(8,128)(2,1)S(1)}, bf16[256,512]{1,0:T(8,128)(2,1)S(1)}, u32[]{:S(2)}, u32[]{:S(2)}) collective-permute-start(bf16[256,512]{1,0:T(8,128)(2,1)S(1)} %collective-permute-done.8.refs_6_.refs_2_), channel_id=1, source_target_pairs={{0,1},{1,0},{2,3},{3,2},{4,5},{5,4},{6,7},{7,6},{8,9},{9,8},{10,11... | collective-permute-start | bytes 786440 | tf_op jit(solution)/shard_map/ppermute | solution.py:271
  25.9 2.3 %collective-permute-done.5.refs_2_ = bf16[144,512]{1,0:T(8,128)(2,1)S(1)} collective-permute-done((bf16[144,512]{1,0:T(8,128)(2,1)S(1)}, bf16[144,512]{1,0:T(8,128)(2,1)S(1)}, u32[]{:S(2)}, u32[]{:S(2)}) %collective-permute-start.5) | collective-permute-done | bytes 147488 | tf_op jit(solution)/shard_map/ppermute | solution.py:271
  28.1 2.0 %collective-permute-done.4.refs_1_ = bf16[144,512]{1,0:T(8,128)(2,1)S(1)} collective-permute-done((bf16[144,512]{1,0:T(8,128)(2,1)S(1)}, bf16[144,512]{1,0:T(8,128)(2,1)S(1)}, u32[]{:S(2)}, u32[]{:S(2)}) %collective-permute-start.4) | collective-permute-done | bytes 147488 | tf_op jit(solution)/shard_map/ppermute | solution.py:271
  31.7 2.1 %shard_map.79 = (f32[128,384]{1,0:T(8,128)S(1)}, bf16[144,384]{1,0:T(8,128)(2,1)S(1)}, bf16[144,384]{1,0:T(8,128)(2,1)S(1)}, bf16[144,384]{1,0:T(8,128)(2,1)S(1)}, f32[8,128]{1,0:T(8,128)S(1)}) custom-call(bf16[1024,384]{1,0:T(8,128)(2,1)S(1)} %bitcast.2, bf16[144,512]{1,0:T(8,128)(2,1)S(1)} %shard_map.77.refs_0_, ...), custom_call_target="tpu_custom_call" | custom-call | tf_op jit(solution)/shard_map/pallas_call | solution.py:46
  34.3 3.9 %collective-permute-start.18 = (bf16[144,384]{1,0:T(8,128)(2,1)S(1)}, bf16[144,384]{1,0:T(8,128)(2,1)S(1)}, u32[]{:S(2)}, u32[]{:S(2)}) collective-permute-start(bf16[144,384]{1,0:T(8,128)(2,1)S(1)} %get-tuple-element.50), channel_id=1, source_target_pairs={{0,3},{1,2},{2,1},{3,0},{4,7},{5,6},{6,5},{7,4},{8,11},{9,10},{10,... | collective-permute-start | bytes 331784 | tf_op jit(solution)/shard_map/ppermute | solution.py:271
  38.8 1.5 %collective-permute-done.16.refs_1_ = bf16[144,384]{1,0:T(8,128)(2,1)S(1)} collective-permute-done((bf16[144,384]{1,0:T(8,128)(2,1)S(1)}, bf16[144,384]{1,0:T(8,128)(2,1)S(1)}, u32[]{:S(2)}, u32[]{:S(2)}) %collective-permute-start.16) | collective-permute-done | bytes 110624 | tf_op jit(solution)/shard_map/ppermute | solution.py:271
  40.2 5.2 %collective-permute-done.17.refs_2_ = bf16[144,384]{1,0:T(8,128)(2,1)S(1)} collective-permute-done((bf16[144,384]{1,0:T(8,128)(2,1)S(1)}, bf16[144,384]{1,0:T(8,128)(2,1)S(1)}, u32[]{:S(2)}, u32[]{:S(2)}) %collective-permute-start.17) | collective-permute-done | bytes 110624 | tf_op jit(solution)/shard_map/ppermute | solution.py:271
  45.8 1.5 %collective-permute-start.21 = (bf16[128,512]{1,0:T(8,128)(2,1)S(1)}, bf16[128,512]{1,0:T(8,128)(2,1)S(1)}, u32[]{:S(2)}, u32[]{:S(2)}) collective-permute-start(bf16[128,512]{1,0:T(8,128)(2,1)S(1)} %get-tuple-element.51.refs_0_), channel_id=1, source_target_pairs={{0,3},{1,2},{2,1},{3,0},{4,7},{5,6},{6,5},{7,4},{8,11},{9,10},{10,... | collective-permute-start | bytes 393224 | tf_op jit(solution)/shard_map/ppermute | solution.py:271
  47.2 2.4 %collective-permute-start.20 = (bf16[128,512]{1,0:T(8,128)(2,1)S(1)}, bf16[128,512]{1,0:T(8,128)(2,1)S(1)}, u32[]{:S(2)}, u32[]{:S(2)}) collective-permute-start(bf16[128,512]{1,0:T(8,128)(2,1)S(1)} %get-tuple-element.51.refs_0_), channel_id=1, source_target_pairs={{0,2},{1,3},{2,0},{3,1},{4,6},{5,7},{6,4},{7,5},{8,10},{9,11},{10,... | collective-permute-start | bytes 393224 | tf_op jit(solution)/shard_map/ppermute | solution.py:271
  50.2 3.8 %collective-permute-done.21.refs_3_ = bf16[128,512]{1,0:T(8,128)(2,1)S(1)} collective-permute-done((bf16[128,512]{1,0:T(8,128)(2,1)S(1)}, bf16[128,512]{1,0:T(8,128)(2,1)S(1)}, u32[]{:S(2)}, u32[]{:S(2)}) %collective-permute-start.21) | collective-permute-done | bytes 131104 | tf_op jit(solution)/shard_map/ppermute | solution.py:271
  54.0 7.8 %collective-permute-done.20.refs_2_ = bf16[128,512]{1,0:T(8,128)(2,1)S(1)} collective-permute-done((bf16[128,512]{1,0:T(8,128)(2,1)S(1)}, bf16[128,512]{1,0:T(8,128)(2,1)S(1)}, u32[]{:S(2)}, u32[]{:S(2)}) %collective-permute-start.20) | collective-permute-done | bytes 131104 | tf_op jit(solution)/shard_map/ppermute | solution.py:271
  61.8 2.9 %shard_map.82 = (bf16[128,256]{1,0:T(8,128)(2,1)S(1)}, bf16[512,384]{1,0:T(8,128)(2,1)S(1)}) custom-call(s32[4,4]{1,0:T(4,128)S(1)} %copy-done.4, bf16[128,512]{1,0:T(8,128)(2,1)S(1)} %get-tuple-element.51.refs_0_, bf16[128,512]{1,0:T(8,128)(2,1)S(1)} %collective-permute-done.19.refs_1_, bf16[128,512]{1,0:T(8,128)(2,1)S(1)} %collective-permute-done.20.refs_2_, ...), custom_call_target="tpu_custom_call" | custom-call | tf_op jit(solution)/shard_map/pallas_call | solution.py:46
  68.1 2.6 %collective-permute-start.30 = (bf16[128,512]{1,0:T(8,128)(2,1)S(1)}, bf16[128,512]{1,0:T(8,128)(2,1)S(1)}, u32[]{:S(2)}, u32[]{:S(2)}) collective-permute-start(bf16[128,512]{1,0:T(8,128)(2,1)S(1)} %get-tuple-element.67), channel_id=1, source_target_pairs={{0,24},{1,25},{2,26},{3,27},{4,28},{5,29},{6,30},{7,31},{8,16},{9,... | collective-permute-start | bytes 393224 | tf_op jit(solution)/shard_map/ppermute | solution.py:271
  72.1 1.5 %collective-permute-done.28.refs_1_ = bf16[128,512]{1,0:T(8,128)(2,1)S(1)} collective-permute-done((bf16[128,512]{1,0:T(8,128)(2,1)S(1)}, bf16[128,512]{1,0:T(8,128)(2,1)S(1)}, u32[]{:S(2)}, u32[]{:S(2)}) %collective-permute-start.28) | collective-permute-done | bytes 131104 | tf_op jit(solution)/shard_map/ppermute | solution.py:271
  75.2 1.4 %collective-permute-done.30.refs_3_ = bf16[128,512]{1,0:T(8,128)(2,1)S(1)} collective-permute-done((bf16[128,512]{1,0:T(8,128)(2,1)S(1)}, bf16[128,512]{1,0:T(8,128)(2,1)S(1)}, u32[]{:S(2)}, u32[]{:S(2)}) %collective-permute-start.30) | collective-permute-done | bytes 131104 | tf_op jit(solution)/shard_map/ppermute | solution.py:271
  76.6 3.4 %collective-permute-start.31 = (bf16[128,512]{1,0:T(8,128)(2,1)S(1)}, bf16[128,512]{1,0:T(8,128)(2,1)S(1)}, u32[]{:S(2)}, u32[]{:S(2)}) collective-permute-start(bf16[128,512]{1,0:T(8,128)(2,1)S(1)} %shard_map.87), channel_id=1, source_target_pairs={{0,0},{1,9},{2,18},{3,27},{4,4},{5,13},{6,22},{7,31},{8,1},{9,8},{... | collective-permute-start | bytes 393224 | tf_op jit(solution)/shard_map/ppermute | solution.py:271
  80.1 2.7 %collective-permute-done.26.refs_3_ = bf16[128,640]{1,0:T(8,128)(2,1)S(1)} collective-permute-done((bf16[128,640]{1,0:T(8,128)(2,1)S(1)}, bf16[128,640]{1,0:T(8,128)(2,1)S(1)}, u32[]{:S(2)}, u32[]{:S(2)}) %collective-permute-start.26) | collective-permute-done | bytes 163872 | tf_op jit(solution)/shard_map/ppermute | solution.py:271
  83.6 3.5 %collective-permute-done.31.grad = bf16[128,512]{1,0:T(8,128)(2,1)S(1)} collective-permute-done((bf16[128,512]{1,0:T(8,128)(2,1)S(1)}, bf16[128,512]{1,0:T(8,128)(2,1)S(1)}, u32[]{:S(2)}, u32[]{:S(2)}) %collective-permute-start.31) | collective-permute-done | bytes 131104 | tf_op jit(solution)/shard_map/ppermute | solution.py:271
  (65 shorter events, 17.4 us)
Async XLA Ops:
  0.6 7.8 %collective-permute-start.7 = (bf16[128,1024]{1,0:T(8,128)(2,1)}, bf16[128,1024]{1,0:T(8,128)(2,1)S(1)}, u32[]{:S(2)}, u32[]{:S(2)}) collective-permute-start(bf16[128,1024]{1,0:T(8,128)(2,1)} %bitcast.5), channel_id=1, source_target_pairs={{0,4},{1,5},{2,6},{3,7},{4,0},{5,1},{6,2},{7,3},{8,12},{9,13},{10,... | collective-permute-start | bytes 786440 | tf_op jit(solution)/shard_map/ppermute | solution.py:271
  0.7 10.5 %collective-permute-start = (bf16[128,512]{1,0:T(8,128)(2,1)}, bf16[128,512]{1,0:T(8,128)(2,1)S(1)}, u32[]{:S(2)}, u32[]{:S(2)}) collective-permute-start(bf16[128,512]{1,0:T(8,128)(2,1)} %x.3), channel_id=1, source_target_pairs={{0,0},{1,8},{2,16},{3,24},{4,4},{5,12},{6,20},{7,28},{8,9},{9,1},{... | collective-permute-start | bytes 393224 | tf_op jit(solution)/shard_map/ppermute | solution.py:271
  4.9 10.1 %collective-permute-start.3 = (bf16[128,512]{1,0:T(8,128)(2,1)}, bf16[128,512]{1,0:T(8,128)(2,1)S(1)}, u32[]{:S(2)}, u32[]{:S(2)}) collective-permute-start(bf16[128,512]{1,0:T(8,128)(2,1)} %cot.1), channel_id=1, source_target_pairs={{0,24},{1,25},{2,26},{3,27},{4,28},{5,29},{6,30},{7,31},{8,16},{9,... | collective-permute-start | bytes 393224 | tf_op jit(solution)/shard_map/ppermute | solution.py:271
  5.8 9.5 %collective-permute-start.2 = (bf16[128,512]{1,0:T(8,128)(2,1)}, bf16[128,512]{1,0:T(8,128)(2,1)S(1)}, u32[]{:S(2)}, u32[]{:S(2)}) collective-permute-start(bf16[128,512]{1,0:T(8,128)(2,1)} %cot.1), channel_id=1, source_target_pairs={{0,16},{1,17},{2,18},{3,19},{4,20},{5,21},{6,22},{7,23},{8,24},{9,... | collective-permute-start | bytes 393224 | tf_op jit(solution)/shard_map/ppermute | solution.py:271
  7.1 8.2 %collective-permute-start.1 = (bf16[128,512]{1,0:T(8,128)(2,1)}, bf16[128,512]{1,0:T(8,128)(2,1)S(1)}, u32[]{:S(2)}, u32[]{:S(2)}) collective-permute-start(bf16[128,512]{1,0:T(8,128)(2,1)} %cot.1), channel_id=1, source_target_pairs={{0,8},{1,9},{2,10},{3,11},{4,12},{5,13},{6,14},{7,15},{8,0},{9,1},... | collective-permute-start | bytes 393224 | tf_op jit(solution)/shard_map/ppermute | solution.py:271
  9.4 13.8 %collective-permute-start.8 = (bf16[256,512]{1,0:T(8,128)(2,1)S(1)}, bf16[256,512]{1,0:T(8,128)(2,1)S(1)}, u32[]{:S(2)}, u32[]{:S(2)}) collective-permute-start(bf16[256,512]{1,0:T(8,128)(2,1)S(1)} %shard_map.78.refs_4_.refs_0_), channel_id=1, source_target_pairs={{0,2},{1,3},{2,0},{3,1},{4,6},{5,7},{6,4},{7,5},{8,10},{9,11},{10,... | collective-permute-start | bytes 786440 | tf_op jit(solution)/shard_map/ppermute | solution.py:271
  15.3 7.5 %collective-permute-start.9 = (bf16[144,512]{1,0:T(8,128)(2,1)S(1)}, bf16[144,512]{1,0:T(8,128)(2,1)S(1)}, u32[]{:S(2)}, u32[]{:S(2)}) collective-permute-start(bf16[144,512]{1,0:T(8,128)(2,1)S(1)} %shard_map.77.refs_0_), channel_id=1, source_target_pairs={{0,4},{1,5},{2,6},{3,7},{4,0},{5,1},{6,2},{7,3},{8,12},{9,13},{10,... | collective-permute-start | bytes 442376 | tf_op jit(solution)/shard_map/ppermute | solution.py:271
  15.3 7.8 %collective-permute-start.6 = (bf16[144,512]{1,0:T(8,128)(2,1)S(1)}, bf16[144,512]{1,0:T(8,128)(2,1)S(1)}, u32[]{:S(2)}, u32[]{:S(2)}) collective-permute-start(bf16[144,512]{1,0:T(8,128)(2,1)S(1)} %shard_map.77.refs_0_), channel_id=1, source_target_pairs={{0,24},{1,25},{2,26},{3,27},{4,28},{5,29},{6,30},{7,31},{8,16},{9,... | collective-permute-start | bytes 442376 | tf_op jit(solution)/shard_map/ppermute | solution.py:271
  17.0 11.1 %collective-permute-start.5 = (bf16[144,512]{1,0:T(8,128)(2,1)S(1)}, bf16[144,512]{1,0:T(8,128)(2,1)S(1)}, u32[]{:S(2)}, u32[]{:S(2)}) collective-permute-start(bf16[144,512]{1,0:T(8,128)(2,1)S(1)} %shard_map.77.refs_0_), channel_id=1, source_target_pairs={{0,16},{1,17},{2,18},{3,19},{4,20},{5,21},{6,22},{7,23},{8,24},{9,... | collective-permute-start | bytes 442376 | tf_op jit(solution)/shard_map/ppermute | solution.py:271
  21.3 8.8 %collective-permute-start.4 = (bf16[144,512]{1,0:T(8,128)(2,1)S(1)}, bf16[144,512]{1,0:T(8,128)(2,1)S(1)}, u32[]{:S(2)}, u32[]{:S(2)}) collective-permute-start(bf16[144,512]{1,0:T(8,128)(2,1)S(1)} %shard_map.77.refs_0_), channel_id=1, source_target_pairs={{0,8},{1,9},{2,10},{3,11},{4,12},{5,13},{6,14},{7,15},{8,0},{9,1},... | collective-permute-start | bytes 442376 | tf_op jit(solution)/shard_map/ppermute | solution.py:271
  22.7 15.5 %collective-permute-start.13 = (bf16[256,512]{1,0:T(8,128)(2,1)S(1)}, bf16[256,512]{1,0:T(8,128)(2,1)S(1)}, u32[]{:S(2)}, u32[]{:S(2)}) collective-permute-start(bf16[256,512]{1,0:T(8,128)(2,1)S(1)} %shard_map.78.refs_4_.refs_0_), channel_id=1, source_target_pairs={{0,1},{1,0},{2,3},{3,2},{4,5},{5,4},{6,7},{7,6},{8,9},{9,8},{10,11... | collective-permute-start | bytes 786440 | tf_op jit(solution)/shard_map/ppermute | solution.py:271
  23.2 15.0 %collective-permute-start.14 = (bf16[256,512]{1,0:T(8,128)(2,1)S(1)}, bf16[256,512]{1,0:T(8,128)(2,1)S(1)}, u32[]{:S(2)}, u32[]{:S(2)}) collective-permute-start(bf16[256,512]{1,0:T(8,128)(2,1)S(1)} %collective-permute-done.8.refs_6_.refs_2_), channel_id=1, source_target_pairs={{0,1},{1,0},{2,3},{3,2},{4,5},{5,4},{6,7},{7,6},{8,9},{9,8},{10,11... | collective-permute-start | bytes 786440 | tf_op jit(solution)/shard_map/ppermute | solution.py:271
  33.8 11.6 %collective-permute-start.17 = (bf16[144,384]{1,0:T(8,128)(2,1)S(1)}, bf16[144,384]{1,0:T(8,128)(2,1)S(1)}, u32[]{:S(2)}, u32[]{:S(2)}) collective-permute-start(bf16[144,384]{1,0:T(8,128)(2,1)S(1)} %get-tuple-element.49), channel_id=1, source_target_pairs={{0,2},{1,3},{2,0},{3,1},{4,6},{5,7},{6,4},{7,5},{8,10},{9,11},{10,... | collective-permute-start | bytes 331784 | tf_op jit(solution)/shard_map/ppermute | solution.py:271
  34.3 11.1 %collective-permute-start.18 = (bf16[144,384]{1,0:T(8,128)(2,1)S(1)}, bf16[144,384]{1,0:T(8,128)(2,1)S(1)}, u32[]{:S(2)}, u32[]{:S(2)}) collective-permute-start(bf16[144,384]{1,0:T(8,128)(2,1)S(1)} %get-tuple-element.50), channel_id=1, source_target_pairs={{0,3},{1,2},{2,1},{3,0},{4,7},{5,6},{6,5},{7,4},{8,11},{9,10},{10,... | collective-permute-start | bytes 331784 | tf_op jit(solution)/shard_map/ppermute | solution.py:271
  45.7 21.0 %collective-permute-start.27 = (bf16[1024,384]{1,0:T(8,128)(2,1)S(1)}, bf16[1024,384]{1,0:T(8,128)(2,1)S(1)}, u32[]{:S(2)}, u32[]{:S(2)}) collective-permute-start(bf16[1024,384]{1,0:T(8,128)(2,1)S(1)} %bitcast.3), channel_id=1, source_target_pairs={{0,4},{1,5},{2,6},{3,7},{4,0},{5,1},{6,2},{7,3},{8,12},{9,13},{10,... | collective-permute-start | bytes 2359304 | tf_op jit(solution)/shard_map/ppermute | solution.py:271
  45.8 8.3 %collective-permute-start.21 = (bf16[128,512]{1,0:T(8,128)(2,1)S(1)}, bf16[128,512]{1,0:T(8,128)(2,1)S(1)}, u32[]{:S(2)}, u32[]{:S(2)}) collective-permute-start(bf16[128,512]{1,0:T(8,128)(2,1)S(1)} %get-tuple-element.51.refs_0_), channel_id=1, source_target_pairs={{0,3},{1,2},{2,1},{3,0},{4,7},{5,6},{6,5},{7,4},{8,11},{9,10},{10,... | collective-permute-start | bytes 393224 | tf_op jit(solution)/shard_map/ppermute | solution.py:271
  47.2 14.6 %collective-permute-start.20 = (bf16[128,512]{1,0:T(8,128)(2,1)S(1)}, bf16[128,512]{1,0:T(8,128)(2,1)S(1)}, u32[]{:S(2)}, u32[]{:S(2)}) collective-permute-start(bf16[128,512]{1,0:T(8,128)(2,1)S(1)} %get-tuple-element.51.refs_0_), channel_id=1, source_target_pairs={{0,2},{1,3},{2,0},{3,1},{4,6},{5,7},{6,4},{7,5},{8,10},{9,11},{10,... | collective-permute-start | bytes 393224 | tf_op jit(solution)/shard_map/ppermute | solution.py:271
  49.6 12.3 %collective-permute-start.19 = (bf16[128,512]{1,0:T(8,128)(2,1)S(1)}, bf16[128,512]{1,0:T(8,128)(2,1)S(1)}, u32[]{:S(2)}, u32[]{:S(2)}) collective-permute-start(bf16[128,512]{1,0:T(8,128)(2,1)S(1)} %get-tuple-element.51.refs_0_), channel_id=1, source_target_pairs={{0,1},{1,0},{2,3},{3,2},{4,5},{5,4},{6,7},{7,6},{8,9},{9,8},{10,11... | collective-permute-start | bytes 393224 | tf_op jit(solution)/shard_map/ppermute | solution.py:271
  67.7 7.5 %collective-permute-start.29 = (bf16[128,512]{1,0:T(8,128)(2,1)S(1)}, bf16[128,512]{1,0:T(8,128)(2,1)S(1)}, u32[]{:S(2)}, u32[]{:S(2)}) collective-permute-start(bf16[128,512]{1,0:T(8,128)(2,1)S(1)} %get-tuple-element.66), channel_id=1, source_target_pairs={{0,16},{1,17},{2,18},{3,19},{4,20},{5,21},{6,22},{7,23},{8,24},{9,... | collective-permute-start | bytes 393224 | tf_op jit(solution)/shard_map/ppermute | solution.py:271
  68.1 8.5 %collective-permute-start.30 = (bf16[128,512]{1,0:T(8,128)(2,1)S(1)}, bf16[128,512]{1,0:T(8,128)(2,1)S(1)}, u32[]{:S(2)}, u32[]{:S(2)}) collective-permute-start(bf16[128,512]{1,0:T(8,128)(2,1)S(1)} %get-tuple-element.67), channel_id=1, source_target_pairs={{0,24},{1,25},{2,26},{3,27},{4,28},{5,29},{6,30},{7,31},{8,16},{9,... | collective-permute-start | bytes 393224 | tf_op jit(solution)/shard_map/ppermute | solution.py:271
  71.2 8.9 %collective-permute-start.24 = (bf16[128,640]{1,0:T(8,128)(2,1)S(1)}, bf16[128,640]{1,0:T(8,128)(2,1)S(1)}, u32[]{:S(2)}, u32[]{:S(2)}) collective-permute-start(bf16[128,640]{1,0:T(8,128)(2,1)S(1)} %get-tuple-element.56), channel_id=1, source_target_pairs={{0,8},{1,9},{2,10},{3,11},{4,12},{5,13},{6,14},{7,15},{8,0},{9,1},... | collective-permute-start | bytes 491528 | tf_op jit(solution)/shard_map/ppermute | solution.py:271
  71.7 8.4 %collective-permute-start.25 = (bf16[128,640]{1,0:T(8,128)(2,1)S(1)}, bf16[128,640]{1,0:T(8,128)(2,1)S(1)}, u32[]{:S(2)}, u32[]{:S(2)}) collective-permute-start(bf16[128,640]{1,0:T(8,128)(2,1)S(1)} %get-tuple-element.57), channel_id=1, source_target_pairs={{0,16},{1,17},{2,18},{3,19},{4,20},{5,21},{6,22},{7,23},{8,24},{9,... | collective-permute-start | bytes 491528 | tf_op jit(solution)/shard_map/ppermute | solution.py:271
  73.6 9.2 %collective-permute-start.26 = (bf16[128,640]{1,0:T(8,128)(2,1)S(1)}, bf16[128,640]{1,0:T(8,128)(2,1)S(1)}, u32[]{:S(2)}, u32[]{:S(2)}) collective-permute-start(bf16[128,640]{1,0:T(8,128)(2,1)S(1)} %get-tuple-element.58), channel_id=1, source_target_pairs={{0,24},{1,25},{2,26},{3,27},{4,28},{5,29},{6,30},{7,31},{8,16},{9,... | collective-permute-start | bytes 491528 | tf_op jit(solution)/shard_map/ppermute | solution.py:271
  76.6 10.5 %collective-permute-start.31 = (bf16[128,512]{1,0:T(8,128)(2,1)S(1)}, bf16[128,512]{1,0:T(8,128)(2,1)S(1)}, u32[]{:S(2)}, u32[]{:S(2)}) collective-permute-start(bf16[128,512]{1,0:T(8,128)(2,1)S(1)} %shard_map.87), channel_id=1, source_target_pairs={{0,0},{1,9},{2,18},{3,27},{4,4},{5,13},{6,22},{7,31},{8,1},{9,8},{... | collective-permute-start | bytes 393224 | tf_op jit(solution)/shard_map/ppermute | solution.py:271
  (14 other events, 90.6 us)

commit v2 on v1

--- a/solution.py
+++ b/solution.py
@@ -57,14 +57,6 @@
     return jax.ShapeDtypeStruct(dims, dtype)
 
 
-def each(n, body):
-    if n <= 4:
-        for e in range(n):
-            body(e)
-    else:
-        lax.fori_loop(0, n, lambda e, carry: (body(e), carry)[1], 0)
-
-
 def stack_kernel(own, sib, out):
     _, core, _ = place()
     rows, feats = own.shape[0], out.shape[1]
@@ -78,50 +70,55 @@
     out[rows:, :] = jnp.broadcast_to(gain[...], (16, feats))
 
 
-def project_kernel(n, w, *refs):
-    same, sib, outs = refs[:n], refs[n : 2 * n], refs[2 * n : 3 * n]
-    own_squares, high, low, held, held_squares = refs[3 * n :]
-    chip, core, plane = place()
-    feats = same[0].shape[1]
-    rows = same[0].shape[0] - 16
-    width = w.shape[1]
-    ones = jnp.ones((8, feats), BF16)
-    line = lax.broadcasted_iota(jnp.int32, (16, rows), 0)
-
-    def parts(value):
-        first = value.astype(BF16)
-        return first, (value - first.astype(F32)).astype(BF16)
-
-    total = jnp.zeros((n * rows, width), F32)
-    def gain_of(blocks):
-        chosen = jnp.zeros((8, feats), F32)
-        for d in range(n):
-            lines = blocks[d][rows:, :].astype(F32)[:8]
-            chosen += jnp.where(jnp.bitwise_xor(chip, d) == plane, lines, 0.0)
-        return chosen[0:1, :]
-
-    gains = gain_of(same), gain_of(sib)
+def gain_of(n, blocks, rows):
+    chip, _, plane = place()
+    chosen = jnp.zeros((8, blocks[0].shape[1]), F32)
+    for d in range(n):
+        lines = blocks[d][rows:, :].astype(F32)[:8]
+        chosen += jnp.where(jnp.bitwise_xor(chip, d) == plane, lines, 0.0)
+    return chosen[0:1, :]
+
+
+def in_parts(value):
+    first = value.astype(BF16)
+    return first, (value - first.astype(F32)).astype(BF16)
+
+
+def project(n, blocks, w, high, low, squares, rows):
+    chip, _, _ = place()
+    gain = gain_of(n, blocks, rows)
+    ones = jnp.ones((8, blocks[0].shape[1]), BF16)
     for d in range(n):
         slot = jnp.bitwise_xor(chip, d)
-        squares = jnp.zeros((8, rows), F32)
-        for i, blocks in enumerate((same, sib)):
-            values = blocks[d][:rows, :].astype(F32)
-            at = (span(slot, rows), slice(i * feats, (i + 1) * feats))
-            high[at], low[at] = parts(values * gains[i])
-            square_high, square_low = parts(values * values)
-            squares += nt(ones, square_high) + nt(ones, square_low)
-        held_squares[slot] = squares
-    w_same, w_sib = w[span(core, feats), :], w[span(1 - core, feats), :]
-    product = nn(high[:, :feats], w_same) + nn(low[:, :feats], w_same)
-    product += nn(high[:, feats:], w_sib) + nn(low[:, feats:], w_sib)
-    held[...] = product
-    outs[0][...] = held[:rows, :]
-    own_squares[...] = held_squares[0]
+        values = blocks[d][:rows, :].astype(F32)
+        high[span(slot, rows), :], low[span(slot, rows), :] = in_parts(values * gain)
+        square_high, square_low = in_parts(values * values)
+        squares[slot] = nt(ones, square_high) + nt(ones, square_low)
+    return nn(high[...], w) + nn(low[...], w)
+
+
+def project_same_kernel(n, w, *refs):
+    blocks, (out, squares, high, low) = refs[:n], refs[n:]
+    _, core, _ = place()
+    rows, feats = squares.shape[2], high.shape[1]
+    out[...] = project(n, blocks, w[span(core, feats), :], high, low, squares, rows)
+
+
+def project_kernel(n, w, same, same_squares, *refs):
+    blocks, outs = refs[:n], refs[n : 2 * n]
+    own_squares, high, low, squares = refs[2 * n :]
+    _, core, _ = place()
+    rows, feats = squares.shape[2], high.shape[1]
+    width = w.shape[1]
+    total = same[...] + project(n, blocks, w[span(1 - core, feats), :], high, low, squares, rows)
+    line = lax.broadcasted_iota(jnp.int32, (16, rows), 0)
+    outs[0][...] = total[:rows]
+    own_squares[...] = same_squares[0] + squares[0]
     for e in range(1, n):
-        outs[e][:rows, :] = held[e * rows : (e + 1) * rows, :].astype(BF16)
-        squares = held_squares[e][0:1, :]
-        first = squares.astype(BF16).astype(F32)
-        stat = jnp.where(line == 0, first, jnp.where(line == 1, squares - first, 0.0))
+        outs[e][:rows, :] = total[e * rows : (e + 1) * rows].astype(BF16)
+        sums = (same_squares[e] + squares[e])[0:1, :]
+        first = sums.astype(BF16).astype(F32)
+        stat = jnp.where(line == 0, first, jnp.where(line == 1, sums - first, 0.0))
         outs[e][rows:, :] = jnp.zeros((16, width), BF16)
         outs[e][rows:, :rows] = stat.astype(BF16)
 
@@ -173,25 +170,27 @@
     value = held[:, 2 * head : 3 * head]
     column_block = lax.broadcasted_iota(jnp.int32, (1, n * rows), 1) // rows
 
-    def one_block(e):
-        at = span(e, rows)
-        row_plane = jnp.bitwise_xor(plane, e)
-        allowed = jnp.zeros((1, n * rows), jnp.int32)
+    def bias(e):
+        line = jnp.zeros((1, n * rows), F32)
         for other in range(n):
-            entry = mask[row_plane, jnp.bitwise_xor(plane, other)]
-            allowed = jnp.where(column_block == other, entry, allowed)
-        scores = jnp.where(allowed > 0, nt(held[at, :head], key) * factor, -1e30)
+            entry = mask[jnp.bitwise_xor(plane, e), jnp.bitwise_xor(plane, other)]
+            line = jnp.where(column_block == other, jnp.where(entry > 0, 0.0, -1e30), line)
+        return jnp.broadcast_to(line, (rows, n * rows))
+
+    together = min(n, 4)
+    for first in range(0, n, together):
+        at = slice(first * rows, (first + together) * rows)
+        masked = jnp.concatenate([bias(first + e) for e in range(together)], axis=0)
+        scores = nt(held[at, :head], key) * factor + masked
         expd = jnp.exp(scores - jnp.max(scores, axis=-1, keepdims=True))
-        probs = expd / jnp.sum(expd, axis=-1, keepdims=True)
-        probs_round = probs.astype(BF16)
+        probs = expd * (1.0 / jnp.sum(expd, axis=-1, keepdims=True))
         d_probs = nt(held[at, 3 * head :], value)
         delta = jnp.sum(probs * d_probs, axis=-1, keepdims=True)
         d_scores = (probs * (d_probs - delta) * factor).astype(BF16)
+        probs_held[at, :] = probs.astype(BF16)
+        d_scores_held[at, :] = d_scores
         d_proj[at, :head] = nn(d_scores, key).astype(BF16)
-        probs_held[at, :] = probs_round
-        d_scores_held[at, :] = d_scores
-
-    each(n, one_block)
+
     d_proj[:, head : 2 * head] = tn(d_scores_held[...], held[:, :head]).astype(BF16)
     d_proj[:, 2 * head :] = tn(probs_held[...], held[:, 3 * head :]).astype(BF16)
     attended_out[:, :head] = nn(probs_held[:rows, :], value).astype(BF16)
@@ -223,11 +222,16 @@
     for e in range(n):
         term = nn(own[:, :head], weights[e][:head, :]) + nn(sib[:, :head], weights[e][head:, :])
         held[jnp.bitwise_xor(turn, e)] = term.astype(BF16)
-    means = own[:, head:].astype(F32) + sib[:, head:].astype(F32)
-    stat = split_stat(jnp.sum(means, axis=1, keepdims=True))
+    rows = own.shape[0]
+    means = jnp.sum(own[:, head:].astype(F32) + sib[:, head:].astype(F32), axis=1, keepdims=True)
+    row = jnp.broadcast_to(means, (rows, rows)).T[:16]
+    first = row.astype(BF16).astype(F32)
+    line = lax.broadcasted_iota(jnp.int32, (16, rows), 0)
+    stat = jnp.where(line == 0, first, jnp.where(line == 1, row - first, 0.0))
     for d in range(n):
-        outs[d][:, :feats] = held[d]
-        outs[d][:, feats:] = stat
+        outs[d][:rows, :] = held[d]
+        outs[d][rows:, :] = jnp.zeros((16, feats), BF16)
+        outs[d][rows:, :rows] = stat.astype(BF16)
 
 
 def sum_kernel(n, *refs):
@@ -239,12 +243,13 @@
 
 def finish_output_kernel(n, x, *refs):
     parts, (out, mean) = refs[:n], refs[n:]
-    feats = x.shape[1]
+    rows = x.shape[0]
     total = parts[0][...].astype(F32)
     for part in parts[1:]:
         total += part[...].astype(F32)
-    out[...] = (x[...].astype(F32) + total[:, :feats]).astype(BF16)
-    mean[...] = jnp.broadcast_to(jnp.sum(total[:, feats:], axis=1, keepdims=True), mean.shape)
+    out[...] = (x[...].astype(F32) + total[:rows]).astype(BF16)
+    row = jnp.sum(total[rows:, :rows], axis=0, keepdims=True)
+    mean[...] = jnp.broadcast_to(row, (rows, rows)).T
 
 
 def finish_grad_kernel(x, gain, cot, root, mean, grad, out):
@@ -287,7 +292,7 @@
 
     x_held = move(activations, lambda c, k, z: (z ^ c, k, c))
     gain = norm_gain.reshape(1, feats)
-    wo_sib = swap(wo)
+    wo_sib, w_sib = lax.optimization_barrier((swap(wo), swap(w)))
     cots = [cotangent] + [to_chip(cotangent, d) for d in range(1, n)]
     own = call(stack_kernel, shape(2 * head, feats), wo, wo_sib)
     order, step = [0, n // 2], n // 2
@@ -297,7 +302,7 @@
     x_same, x_sib = [x_held], [swap(x_held)]
     for d in range(1, n):
         block = to_chip(x_held, d)
-        if d == min(3, n - 1):
+        if d == min(1, n - 1):
             block, far = lax.optimization_barrier((block, far))
         x_same.append(block)
         x_sib.append(swap(block))
@@ -307,18 +312,20 @@
         ready = [after(part, x_sib[0 if i == 0 else 0]) for i, part in enumerate(weights)]
         weights += [to_plane(part, step) for part in ready]
         order += [o ^ step for o in order]
+    work = [pltpu.VMEM((tokens, feats), BF16)] * 2
+    same, squares = call(
+        functools.partial(project_same_kernel, n),
+        (shape(tokens, width, dtype=F32), shape(n, 8, rows, dtype=F32)),
+        w, *x_same,
+        scratch=work,
+    )
     *parts, own_squares = call(
         functools.partial(project_kernel, n),
         [shape(rows, width, dtype=F32)]
         + [shape(rows + 16, width)] * (n - 1)
         + [shape(8, rows, dtype=F32)],
-        w, *x_same, *x_sib,
-        scratch=[
-            pltpu.VMEM((n * rows, 2 * feats), BF16),
-            pltpu.VMEM((n * rows, 2 * feats), BF16),
-            pltpu.VMEM((n * rows, width), F32),
-            pltpu.VMEM((n, 8, rows), F32),
-        ],
+        w, same, squares, *x_sib,
+        scratch=work + [pltpu.VMEM((n, 8, rows), F32)],
     )
     parts = [parts[0]] + [to_plane(parts[e], e) for e in range(1, n)]
 
@@ -333,9 +340,8 @@
     mixed, root = call(
         functools.partial(combine_kernel, n, features),
         (shape(rows, width + head), shape(rows, rows, dtype=F32)),
-        own_squares, d_att, d_att_sib, *parts,
-    )
-    w_sib = swap(after(w, mixed))
+        own_squares, d_att, d_att_sib, parts[0], *parts[:0:-1],
+    )
     mixed = [mixed] + [to_plane(mixed, e) for e in range(1, n)]
     attended, d_proj = call(
         functools.partial(attention_kernel, n, features),
@@ -359,7 +365,7 @@
     grads = [grads[0]] + [to_chip(grads[d], d) for d in range(1, n)]
     terms = call(
         functools.partial(term_kernel, n),
-        [shape(rows, feats + STAT)] * n,
+        [shape(rows + 16, feats)] * n,
         attended, attended_sib, *weights,
         scratch=[pltpu.VMEM((n, rows, feats), BF16)],
     )
@@ -368,7 +374,7 @@
     grad = move(grad, lambda c, k, z: (z, k, z ^ c))
     output, mean = call(
         functools.partial(finish_output_kernel, n),
-        (shape(rows, feats), shape(rows, STAT, dtype=F32)),
+        (shape(rows, feats), shape(rows, rows, dtype=F32)),
         activations, *terms,
     )
     input_grad = call(

time: 88.1 us -> 84.1 us (0.955)
  waiting for transfers between devices: 39.7 us -> 35.8 us
    ppermute x32, waiting for transfers between devices: 39.7 us -> 35.8 us  [move(): return lax.ppermute(value, AXES, pairs)]
    pallas_call x12 -> x13, Pallas kernels: 8.72 us -> 8.05 us  [call(): pl.pallas_call(kernel, out_shape=out_shape, in_specs=specs, out_specs=jax...]
  transfers between devices with their start and end apart: 32 -> 32, of which waited for: 18 -> 16; matrix products, arithmetic and copies ran while one was open for 0% -> 0% of each run, Pallas kernels for 8% -> 6%
where the time goes in v2:
time: 84.1 us; the launch traced here: 83.6 us
  starting transfers between devices  37.6 us (45%)
  waiting for transfers between devices  35.8 us (43%)
  Pallas kernels  8.05 us (10%)
  local copies, waits for them, and re-layouts  1.25 us (1%)
  between operations  0.85 us (1%)
    ppermute x32, starting transfers between devices, move(): return lax.ppermute(value, AXES, pairs)  37.6 us
    ppermute x32, waiting for transfers between devices, move(): return lax.ppermute(value, AXES, pairs)  35.8 us
    pallas_call x13, Pallas kernels, call(): pl.pallas_call(kernel, out_shape=out_shape, in_specs=specs, out_specs=jax...  8.05 us
  transfers between devices with their start and end apart: 32, of which 16 were waited for; matrix products, arithmetic and copies ran while one was open for 0% of the time, Pallas kernels for 6%

profile of v2, /device:TPU:24, one launch (start us, length us, event | category | flops | bytes accessed | tf_op | source)
XLA Modules:
  0.0 83.6 jit_solution(12595425365230012832)
XLA Ops:
  1.2 4.0 %collective-permute-start = (bf16[128,512]{1,0:T(8,128)(2,1)}, bf16[128,512]{1,0:T(8,128)(2,1)S(1)}, u32[]{:S(2)}, u32[]{:S(2)}) collective-permute-start(bf16[128,512]{1,0:T(8,128)(2,1)} %x.3), channel_id=1, source_target_pairs={{0,0},{1,8},{2,16},{3,24},{4,4},{5,12},{6,20},{7,28},{8,9},{9,1},{... | collective-permute-start | bytes 393224 | tf_op jit(solution)/shard_map/ppermute | solution.py:276
  6.7 2.1 %collective-permute-start.3 = (bf16[128,512]{1,0:T(8,128)(2,1)}, bf16[128,512]{1,0:T(8,128)(2,1)S(1)}, u32[]{:S(2)}, u32[]{:S(2)}) collective-permute-start(bf16[128,512]{1,0:T(8,128)(2,1)} %cot.1), channel_id=1, source_target_pairs={{0,24},{1,25},{2,26},{3,27},{4,28},{5,29},{6,30},{7,31},{8,16},{9,... | collective-permute-start | bytes 393224 | tf_op jit(solution)/shard_map/ppermute | solution.py:276
  10.4 1.2 %collective-permute-done.x = bf16[128,512]{1,0:T(8,128)(2,1)S(1)} collective-permute-done((bf16[128,512]{1,0:T(8,128)(2,1)}, bf16[128,512]{1,0:T(8,128)(2,1)S(1)}, u32[]{:S(2)}, u32[]{:S(2)}) %collective-permute-start) | collective-permute-done | bytes 131104 | tf_op jit(solution)/shard_map/ppermute | solution.py:276
  12.5 4.8 %collective-permute-done.3.refs_3_ = bf16[128,512]{1,0:T(8,128)(2,1)S(1)} collective-permute-done((bf16[128,512]{1,0:T(8,128)(2,1)}, bf16[128,512]{1,0:T(8,128)(2,1)S(1)}, u32[]{:S(2)}, u32[]{:S(2)}) %collective-permute-start.3) | collective-permute-done | bytes 131104 | tf_op jit(solution)/shard_map/ppermute | solution.py:276
  17.4 4.3 %collective-permute-start.8 = (bf16[144,512]{1,0:T(8,128)(2,1)S(1)}, bf16[144,512]{1,0:T(8,128)(2,1)S(1)}, u32[]{:S(2)}, u32[]{:S(2)}) collective-permute-start(bf16[144,512]{1,0:T(8,128)(2,1)S(1)} %shard_map.77.refs_0_), channel_id=1, source_target_pairs={{0,16},{1,17},{2,18},{3,19},{4,20},{5,21},{6,22},{7,23},{8,24},{9,... | collective-permute-start | bytes 442376 | tf_op jit(solution)/shard_map/ppermute | solution.py:276
  21.7 1.4 %collective-permute-start.9 = (bf16[144,512]{1,0:T(8,128)(2,1)S(1)}, bf16[144,512]{1,0:T(8,128)(2,1)S(1)}, u32[]{:S(2)}, u32[]{:S(2)}) collective-permute-start(bf16[144,512]{1,0:T(8,128)(2,1)S(1)} %shard_map.77.refs_0_), channel_id=1, source_target_pairs={{0,24},{1,25},{2,26},{3,27},{4,28},{5,29},{6,30},{7,31},{8,16},{9,... | collective-permute-start | bytes 442376 | tf_op jit(solution)/shard_map/ppermute | solution.py:276
  23.6 1.5 %collective-permute-start.15 = (bf16[256,512]{1,0:T(8,128)(2,1)S(1)}, bf16[256,512]{1,0:T(8,128)(2,1)S(1)}, u32[]{:S(2)}, u32[]{:S(2)}) collective-permute-start(bf16[256,512]{1,0:T(8,128)(2,1)S(1)} %collective-permute-done.7.refs_6_.refs_2_), channel_id=1, source_target_pairs={{0,1},{1,0},{2,3},{3,2},{4,5},{5,4},{6,7},{7,6},{8,9},{9,8},{10,11... | collective-permute-start | bytes 786440 | tf_op jit(solution)/shard_map/ppermute | solution.py:276
  25.1 3.4 %collective-permute-done.8.refs_2_ = bf16[144,512]{1,0:T(8,128)(2,1)S(1)} collective-permute-done((bf16[144,512]{1,0:T(8,128)(2,1)S(1)}, bf16[144,512]{1,0:T(8,128)(2,1)S(1)}, u32[]{:S(2)}, u32[]{:S(2)}) %collective-permute-start.8) | collective-permute-done | bytes 147488 | tf_op jit(solution)/shard_map/ppermute | solution.py:276
  28.5 1.9 %collective-permute-done.9.refs_3_ = bf16[144,512]{1,0:T(8,128)(2,1)S(1)} collective-permute-done((bf16[144,512]{1,0:T(8,128)(2,1)S(1)}, bf16[144,512]{1,0:T(8,128)(2,1)S(1)}, u32[]{:S(2)}, u32[]{:S(2)}) %collective-permute-start.9) | collective-permute-done | bytes 147488 | tf_op jit(solution)/shard_map/ppermute | solution.py:276
  33.9 3.9 %collective-permute-start.19 = (bf16[144,384]{1,0:T(8,128)(2,1)S(1)}, bf16[144,384]{1,0:T(8,128)(2,1)S(1)}, u32[]{:S(2)}, u32[]{:S(2)}) collective-permute-start(bf16[144,384]{1,0:T(8,128)(2,1)S(1)} %get-tuple-element.56), channel_id=1, source_target_pairs={{0,1},{1,0},{2,3},{3,2},{4,5},{5,4},{6,7},{7,6},{8,9},{9,8},{10,11... | collective-permute-start | bytes 331784 | tf_op jit(solution)/shard_map/ppermute | solution.py:276
  38.3 2.8 %collective-permute-done.17.refs_1_ = bf16[144,384]{1,0:T(8,128)(2,1)S(1)} collective-permute-done((bf16[144,384]{1,0:T(8,128)(2,1)S(1)}, bf16[144,384]{1,0:T(8,128)(2,1)S(1)}, u32[]{:S(2)}, u32[]{:S(2)}) %collective-permute-start.17) | collective-permute-done | bytes 110624 | tf_op jit(solution)/shard_map/ppermute | solution.py:276
  41.2 3.1 %collective-permute-done.18.refs_2_ = bf16[144,384]{1,0:T(8,128)(2,1)S(1)} collective-permute-done((bf16[144,384]{1,0:T(8,128)(2,1)S(1)}, bf16[144,384]{1,0:T(8,128)(2,1)S(1)}, u32[]{:S(2)}, u32[]{:S(2)}) %collective-permute-start.18) | collective-permute-done | bytes 110624 | tf_op jit(solution)/shard_map/ppermute | solution.py:276
  44.6 2.5 %collective-permute-start.21 = (bf16[128,512]{1,0:T(8,128)(2,1)S(1)}, bf16[128,512]{1,0:T(8,128)(2,1)S(1)}, u32[]{:S(2)}, u32[]{:S(2)}) collective-permute-start(bf16[128,512]{1,0:T(8,128)(2,1)S(1)} %get-tuple-element.57.refs_0_), channel_id=1, source_target_pairs={{0,2},{1,3},{2,0},{3,1},{4,6},{5,7},{6,4},{7,5},{8,10},{9,11},{10,... | collective-permute-start | bytes 393224 | tf_op jit(solution)/shard_map/ppermute | solution.py:276
  47.1 1.9 %collective-permute-start.22 = (bf16[128,512]{1,0:T(8,128)(2,1)S(1)}, bf16[128,512]{1,0:T(8,128)(2,1)S(1)}, u32[]{:S(2)}, u32[]{:S(2)}) collective-permute-start(bf16[128,512]{1,0:T(8,128)(2,1)S(1)} %get-tuple-element.57.refs_0_), channel_id=1, source_target_pairs={{0,3},{1,2},{2,1},{3,0},{4,7},{5,6},{6,5},{7,4},{8,11},{9,10},{10,... | collective-permute-start | bytes 393224 | tf_op jit(solution)/shard_map/ppermute | solution.py:276
  49.0 2.3 %collective-permute-done.20.refs_1_ = bf16[128,512]{1,0:T(8,128)(2,1)S(1)} collective-permute-done((bf16[128,512]{1,0:T(8,128)(2,1)S(1)}, bf16[128,512]{1,0:T(8,128)(2,1)S(1)}, u32[]{:S(2)}, u32[]{:S(2)}) %collective-permute-start.20) | collective-permute-done | bytes 131104 | tf_op jit(solution)/shard_map/ppermute | solution.py:276
  51.2 6.2 %collective-permute-done.21.refs_2_ = bf16[128,512]{1,0:T(8,128)(2,1)S(1)} collective-permute-done((bf16[128,512]{1,0:T(8,128)(2,1)S(1)}, bf16[128,512]{1,0:T(8,128)(2,1)S(1)}, u32[]{:S(2)}, u32[]{:S(2)}) %collective-permute-start.21) | collective-permute-done | bytes 131104 | tf_op jit(solution)/shard_map/ppermute | solution.py:276
  57.4 2.0 %shard_map.83 = (bf16[128,256]{1,0:T(8,128)(2,1)S(1)}, bf16[512,384]{1,0:T(8,128)(2,1)S(1)}) custom-call(s32[4,4]{1,0:T(4,128)S(1)} %copy-done.4, bf16[128,512]{1,0:T(8,128)(2,1)S(1)} %get-tuple-element.57.refs_0_, bf16[128,512]{1,0:T(8,128)(2,1)S(1)} %collective-permute-done.20.refs_1_, bf16[128,512]{1,0:T(8,128)(2,1)S(1)} %collective-permute-done.21.refs_2_, ...), custom_call_target="tpu_custom_call" | custom-call | tf_op jit(solution)/shard_map/pallas_call | solution.py:46
  62.9 1.7 %collective-permute-start.29 = (bf16[128,512]{1,0:T(8,128)(2,1)S(1)}, bf16[128,512]{1,0:T(8,128)(2,1)S(1)}, u32[]{:S(2)}, u32[]{:S(2)}) collective-permute-start(bf16[128,512]{1,0:T(8,128)(2,1)S(1)} %get-tuple-element.72), channel_id=1, source_target_pairs={{0,16},{1,17},{2,18},{3,19},{4,20},{5,21},{6,22},{7,23},{8,24},{9,... | collective-permute-start | bytes 393224 | tf_op jit(solution)/shard_map/ppermute | solution.py:276
  66.9 1.7 %collective-permute-start.26 = (bf16[144,512]{1,0:T(8,128)(2,1)S(1)}, bf16[144,512]{1,0:T(8,128)(2,1)S(1)}, u32[]{:S(2)}, u32[]{:S(2)}) collective-permute-start(bf16[144,512]{1,0:T(8,128)(2,1)S(1)} %get-tuple-element.63), channel_id=1, source_target_pairs={{0,16},{1,17},{2,18},{3,19},{4,20},{5,21},{6,22},{7,23},{8,24},{9,... | collective-permute-start | bytes 442376 | tf_op jit(solution)/shard_map/ppermute | solution.py:276
  68.6 1.8 %collective-permute-start.27 = (bf16[144,512]{1,0:T(8,128)(2,1)S(1)}, bf16[144,512]{1,0:T(8,128)(2,1)S(1)}, u32[]{:S(2)}, u32[]{:S(2)}) collective-permute-start(bf16[144,512]{1,0:T(8,128)(2,1)S(1)} %get-tuple-element.64), channel_id=1, source_target_pairs={{0,24},{1,25},{2,26},{3,27},{4,28},{5,29},{6,30},{7,31},{8,16},{9,... | collective-permute-start | bytes 442376 | tf_op jit(solution)/shard_map/ppermute | solution.py:276
  71.0 1.2 %collective-permute-done.30.refs_3_ = bf16[128,512]{1,0:T(8,128)(2,1)S(1)} collective-permute-done((bf16[128,512]{1,0:T(8,128)(2,1)S(1)}, bf16[128,512]{1,0:T(8,128)(2,1)S(1)}, u32[]{:S(2)}, u32[]{:S(2)}) %collective-permute-start.30) | collective-permute-done | bytes 131104 | tf_op jit(solution)/shard_map/ppermute | solution.py:276
  72.3 3.6 %collective-permute-start.31 = (bf16[128,512]{1,0:T(8,128)(2,1)S(1)}, bf16[128,512]{1,0:T(8,128)(2,1)S(1)}, u32[]{:S(2)}, u32[]{:S(2)}) collective-permute-start(bf16[128,512]{1,0:T(8,128)(2,1)S(1)} %shard_map.88), channel_id=1, source_target_pairs={{0,0},{1,9},{2,18},{3,27},{4,4},{5,13},{6,22},{7,31},{8,1},{9,8},{... | collective-permute-start | bytes 393224 | tf_op jit(solution)/shard_map/ppermute | solution.py:276
  76.0 2.0 %collective-permute-done.26.refs_2_ = bf16[144,512]{1,0:T(8,128)(2,1)S(1)} collective-permute-done((bf16[144,512]{1,0:T(8,128)(2,1)S(1)}, bf16[144,512]{1,0:T(8,128)(2,1)S(1)}, u32[]{:S(2)}, u32[]{:S(2)}) %collective-permute-start.26) | collective-permute-done | bytes 147488 | tf_op jit(solution)/shard_map/ppermute | solution.py:276
  78.7 4.1 %collective-permute-done.31.grad = bf16[128,512]{1,0:T(8,128)(2,1)S(1)} collective-permute-done((bf16[128,512]{1,0:T(8,128)(2,1)S(1)}, bf16[128,512]{1,0:T(8,128)(2,1)S(1)}, u32[]{:S(2)}, u32[]{:S(2)}) %collective-permute-start.31) | collective-permute-done | bytes 131104 | tf_op jit(solution)/shard_map/ppermute | solution.py:276
  (66 shorter events, 17.5 us)
Async XLA Ops:
  0.6 8.1 %collective-permute-start.6 = (bf16[1024,384]{1,0:T(8,128)(2,1)}, bf16[1024,384]{1,0:T(8,128)(2,1)S(1)}, u32[]{:S(2)}, u32[]{:S(2)}) collective-permute-start(bf16[1024,384]{1,0:T(8,128)(2,1)} %bitcast.2), channel_id=1, source_target_pairs={{0,4},{1,5},{2,6},{3,7},{4,0},{5,1},{6,2},{7,3},{8,12},{9,13},{10,... | collective-permute-start | bytes 2359304 | tf_op jit(solution)/shard_map/ppermute | solution.py:276
  1.2 10.4 %collective-permute-start = (bf16[128,512]{1,0:T(8,128)(2,1)}, bf16[128,512]{1,0:T(8,128)(2,1)S(1)}, u32[]{:S(2)}, u32[]{:S(2)}) collective-permute-start(bf16[128,512]{1,0:T(8,128)(2,1)} %x.3), channel_id=1, source_target_pairs={{0,0},{1,8},{2,16},{3,24},{4,4},{5,12},{6,20},{7,28},{8,9},{9,1},{... | collective-permute-start | bytes 393224 | tf_op jit(solution)/shard_map/ppermute | solution.py:276
  5.2 6.7 %collective-permute-start.1 = (bf16[128,512]{1,0:T(8,128)(2,1)}, bf16[128,512]{1,0:T(8,128)(2,1)S(1)}, u32[]{:S(2)}, u32[]{:S(2)}) collective-permute-start(bf16[128,512]{1,0:T(8,128)(2,1)} %cot.1), channel_id=1, source_target_pairs={{0,8},{1,9},{2,10},{3,11},{4,12},{5,13},{6,14},{7,15},{8,0},{9,1},... | collective-permute-start | bytes 393224 | tf_op jit(solution)/shard_map/ppermute | solution.py:276
  5.9 6.6 %collective-permute-start.2 = (bf16[128,512]{1,0:T(8,128)(2,1)}, bf16[128,512]{1,0:T(8,128)(2,1)S(1)}, u32[]{:S(2)}, u32[]{:S(2)}) collective-permute-start(bf16[128,512]{1,0:T(8,128)(2,1)} %cot.1), channel_id=1, source_target_pairs={{0,16},{1,17},{2,18},{3,19},{4,20},{5,21},{6,22},{7,23},{8,24},{9,... | collective-permute-start | bytes 393224 | tf_op jit(solution)/shard_map/ppermute | solution.py:276
  6.7 10.6 %collective-permute-start.3 = (bf16[128,512]{1,0:T(8,128)(2,1)}, bf16[128,512]{1,0:T(8,128)(2,1)S(1)}, u32[]{:S(2)}, u32[]{:S(2)}) collective-permute-start(bf16[128,512]{1,0:T(8,128)(2,1)} %cot.1), channel_id=1, source_target_pairs={{0,24},{1,25},{2,26},{3,27},{4,28},{5,29},{6,30},{7,31},{8,16},{9,... | collective-permute-start | bytes 393224 | tf_op jit(solution)/shard_map/ppermute | solution.py:276
  9.8 13.9 %collective-permute-start.7 = (bf16[256,512]{1,0:T(8,128)(2,1)S(1)}, bf16[256,512]{1,0:T(8,128)(2,1)S(1)}, u32[]{:S(2)}, u32[]{:S(2)}) collective-permute-start(bf16[256,512]{1,0:T(8,128)(2,1)S(1)} %shard_map.78.refs_4_.refs_0_), channel_id=1, source_target_pairs={{0,2},{1,3},{2,0},{3,1},{4,6},{5,7},{6,4},{7,5},{8,10},{9,11},{10,... | collective-permute-start | bytes 786440 | tf_op jit(solution)/shard_map/ppermute | solution.py:276
  17.4 6.3 %collective-permute-start.4 = (bf16[144,512]{1,0:T(8,128)(2,1)S(1)}, bf16[144,512]{1,0:T(8,128)(2,1)S(1)}, u32[]{:S(2)}, u32[]{:S(2)}) collective-permute-start(bf16[144,512]{1,0:T(8,128)(2,1)S(1)} %shard_map.77.refs_0_), channel_id=1, source_target_pairs={{0,8},{1,9},{2,10},{3,11},{4,12},{5,13},{6,14},{7,15},{8,0},{9,1},... | collective-permute-start | bytes 442376 | tf_op jit(solution)/shard_map/ppermute | solution.py:276
  17.4 11.1 %collective-permute-start.8 = (bf16[144,512]{1,0:T(8,128)(2,1)S(1)}, bf16[144,512]{1,0:T(8,128)(2,1)S(1)}, u32[]{:S(2)}, u32[]{:S(2)}) collective-permute-start(bf16[144,512]{1,0:T(8,128)(2,1)S(1)} %shard_map.77.refs_0_), channel_id=1, source_target_pairs={{0,16},{1,17},{2,18},{3,19},{4,20},{5,21},{6,22},{7,23},{8,24},{9,... | collective-permute-start | bytes 442376 | tf_op jit(solution)/shard_map/ppermute | solution.py:276
  21.7 8.7 %collective-permute-start.9 = (bf16[144,512]{1,0:T(8,128)(2,1)S(1)}, bf16[144,512]{1,0:T(8,128)(2,1)S(1)}, u32[]{:S(2)}, u32[]{:S(2)}) collective-permute-start(bf16[144,512]{1,0:T(8,128)(2,1)S(1)} %shard_map.77.refs_0_), channel_id=1, source_target_pairs={{0,24},{1,25},{2,26},{3,27},{4,28},{5,29},{6,30},{7,31},{8,16},{9,... | collective-permute-start | bytes 442376 | tf_op jit(solution)/shard_map/ppermute | solution.py:276
  23.1 14.7 %collective-permute-start.14 = (bf16[256,512]{1,0:T(8,128)(2,1)S(1)}, bf16[256,512]{1,0:T(8,128)(2,1)S(1)}, u32[]{:S(2)}, u32[]{:S(2)}) collective-permute-start(bf16[256,512]{1,0:T(8,128)(2,1)S(1)} %shard_map.78.refs_4_.refs_0_), channel_id=1, source_target_pairs={{0,1},{1,0},{2,3},{3,2},{4,5},{5,4},{6,7},{7,6},{8,9},{9,8},{10,11... | collective-permute-start | bytes 786440 | tf_op jit(solution)/shard_map/ppermute | solution.py:276
  23.6 14.2 %collective-permute-start.15 = (bf16[256,512]{1,0:T(8,128)(2,1)S(1)}, bf16[256,512]{1,0:T(8,128)(2,1)S(1)}, u32[]{:S(2)}, u32[]{:S(2)}) collective-permute-start(bf16[256,512]{1,0:T(8,128)(2,1)S(1)} %collective-permute-done.7.refs_6_.refs_2_), channel_id=1, source_target_pairs={{0,1},{1,0},{2,3},{3,2},{4,5},{5,4},{6,7},{7,6},{8,9},{9,8},{10,11... | collective-permute-start | bytes 786440 | tf_op jit(solution)/shard_map/ppermute | solution.py:276
  33.3 7.9 %collective-permute-start.17 = (bf16[144,384]{1,0:T(8,128)(2,1)S(1)}, bf16[144,384]{1,0:T(8,128)(2,1)S(1)}, u32[]{:S(2)}, u32[]{:S(2)}) collective-permute-start(bf16[144,384]{1,0:T(8,128)(2,1)S(1)} %get-tuple-element.54), channel_id=1, source_target_pairs={{0,3},{1,2},{2,1},{3,0},{4,7},{5,6},{6,5},{7,4},{8,11},{9,10},{10,... | collective-permute-start | bytes 331784 | tf_op jit(solution)/shard_map/ppermute | solution.py:276
  33.4 10.9 %collective-permute-start.18 = (bf16[144,384]{1,0:T(8,128)(2,1)S(1)}, bf16[144,384]{1,0:T(8,128)(2,1)S(1)}, u32[]{:S(2)}, u32[]{:S(2)}) collective-permute-start(bf16[144,384]{1,0:T(8,128)(2,1)S(1)} %get-tuple-element.55), channel_id=1, source_target_pairs={{0,2},{1,3},{2,0},{3,1},{4,6},{5,7},{6,4},{7,5},{8,10},{9,11},{10,... | collective-permute-start | bytes 331784 | tf_op jit(solution)/shard_map/ppermute | solution.py:276
  33.9 10.4 %collective-permute-start.19 = (bf16[144,384]{1,0:T(8,128)(2,1)S(1)}, bf16[144,384]{1,0:T(8,128)(2,1)S(1)}, u32[]{:S(2)}, u32[]{:S(2)}) collective-permute-start(bf16[144,384]{1,0:T(8,128)(2,1)S(1)} %get-tuple-element.56), channel_id=1, source_target_pairs={{0,1},{1,0},{2,3},{3,2},{4,5},{5,4},{6,7},{7,6},{8,9},{9,8},{10,11... | collective-permute-start | bytes 331784 | tf_op jit(solution)/shard_map/ppermute | solution.py:276
  44.5 6.8 %collective-permute-start.20 = (bf16[128,512]{1,0:T(8,128)(2,1)S(1)}, bf16[128,512]{1,0:T(8,128)(2,1)S(1)}, u32[]{:S(2)}, u32[]{:S(2)}) collective-permute-start(bf16[128,512]{1,0:T(8,128)(2,1)S(1)} %get-tuple-element.57.refs_0_), channel_id=1, source_target_pairs={{0,1},{1,0},{2,3},{3,2},{4,5},{5,4},{6,7},{7,6},{8,9},{9,8},{10,11... | collective-permute-start | bytes 393224 | tf_op jit(solution)/shard_map/ppermute | solution.py:276
  44.6 12.8 %collective-permute-start.21 = (bf16[128,512]{1,0:T(8,128)(2,1)S(1)}, bf16[128,512]{1,0:T(8,128)(2,1)S(1)}, u32[]{:S(2)}, u32[]{:S(2)}) collective-permute-start(bf16[128,512]{1,0:T(8,128)(2,1)S(1)} %get-tuple-element.57.refs_0_), channel_id=1, source_target_pairs={{0,2},{1,3},{2,0},{3,1},{4,6},{5,7},{6,4},{7,5},{8,10},{9,11},{10,... | collective-permute-start | bytes 393224 | tf_op jit(solution)/shard_map/ppermute | solution.py:276
  47.1 10.3 %collective-permute-start.22 = (bf16[128,512]{1,0:T(8,128)(2,1)S(1)}, bf16[128,512]{1,0:T(8,128)(2,1)S(1)}, u32[]{:S(2)}, u32[]{:S(2)}) collective-permute-start(bf16[128,512]{1,0:T(8,128)(2,1)S(1)} %get-tuple-element.57.refs_0_), channel_id=1, source_target_pairs={{0,3},{1,2},{2,1},{3,0},{4,7},{5,6},{6,5},{7,4},{8,11},{9,10},{10,... | collective-permute-start | bytes 393224 | tf_op jit(solution)/shard_map/ppermute | solution.py:276
  61.8 6.8 %collective-permute-start.28 = (bf16[128,512]{1,0:T(8,128)(2,1)S(1)}, bf16[128,512]{1,0:T(8,128)(2,1)S(1)}, u32[]{:S(2)}, u32[]{:S(2)}) collective-permute-start(bf16[128,512]{1,0:T(8,128)(2,1)S(1)} %get-tuple-element.71), channel_id=1, source_target_pairs={{0,8},{1,9},{2,10},{3,11},{4,12},{5,13},{6,14},{7,15},{8,0},{9,1},... | collective-permute-start | bytes 393224 | tf_op jit(solution)/shard_map/ppermute | solution.py:276
  62.9 8.2 %collective-permute-start.29 = (bf16[128,512]{1,0:T(8,128)(2,1)S(1)}, bf16[128,512]{1,0:T(8,128)(2,1)S(1)}, u32[]{:S(2)}, u32[]{:S(2)}) collective-permute-start(bf16[128,512]{1,0:T(8,128)(2,1)S(1)} %get-tuple-element.72), channel_id=1, source_target_pairs={{0,16},{1,17},{2,18},{3,19},{4,20},{5,21},{6,22},{7,23},{8,24},{9,... | collective-permute-start | bytes 393224 | tf_op jit(solution)/shard_map/ppermute | solution.py:276
  64.6 7.6 %collective-permute-start.30 = (bf16[128,512]{1,0:T(8,128)(2,1)S(1)}, bf16[128,512]{1,0:T(8,128)(2,1)S(1)}, u32[]{:S(2)}, u32[]{:S(2)}) collective-permute-start(bf16[128,512]{1,0:T(8,128)(2,1)S(1)} %get-tuple-element.73), channel_id=1, source_target_pairs={{0,24},{1,25},{2,26},{3,27},{4,28},{5,29},{6,30},{7,31},{8,16},{9,... | collective-permute-start | bytes 393224 | tf_op jit(solution)/shard_map/ppermute | solution.py:276
  65.8 10.2 %collective-permute-start.25 = (bf16[144,512]{1,0:T(8,128)(2,1)S(1)}, bf16[144,512]{1,0:T(8,128)(2,1)S(1)}, u32[]{:S(2)}, u32[]{:S(2)}) collective-permute-start(bf16[144,512]{1,0:T(8,128)(2,1)S(1)} %get-tuple-element.62), channel_id=1, source_target_pairs={{0,8},{1,9},{2,10},{3,11},{4,12},{5,13},{6,14},{7,15},{8,0},{9,1},... | collective-permute-start | bytes 442376 | tf_op jit(solution)/shard_map/ppermute | solution.py:276
  66.9 11.0 %collective-permute-start.26 = (bf16[144,512]{1,0:T(8,128)(2,1)S(1)}, bf16[144,512]{1,0:T(8,128)(2,1)S(1)}, u32[]{:S(2)}, u32[]{:S(2)}) collective-permute-start(bf16[144,512]{1,0:T(8,128)(2,1)S(1)} %get-tuple-element.63), channel_id=1, source_target_pairs={{0,16},{1,17},{2,18},{3,19},{4,20},{5,21},{6,22},{7,23},{8,24},{9,... | collective-permute-start | bytes 442376 | tf_op jit(solution)/shard_map/ppermute | solution.py:276
  68.6 9.3 %collective-permute-start.27 = (bf16[144,512]{1,0:T(8,128)(2,1)S(1)}, bf16[144,512]{1,0:T(8,128)(2,1)S(1)}, u32[]{:S(2)}, u32[]{:S(2)}) collective-permute-start(bf16[144,512]{1,0:T(8,128)(2,1)S(1)} %get-tuple-element.64), channel_id=1, source_target_pairs={{0,24},{1,25},{2,26},{3,27},{4,28},{5,29},{6,30},{7,31},{8,16},{9,... | collective-permute-start | bytes 442376 | tf_op jit(solution)/shard_map/ppermute | solution.py:276
  72.3 10.6 %collective-permute-start.31 = (bf16[128,512]{1,0:T(8,128)(2,1)S(1)}, bf16[128,512]{1,0:T(8,128)(2,1)S(1)}, u32[]{:S(2)}, u32[]{:S(2)}) collective-permute-start(bf16[128,512]{1,0:T(8,128)(2,1)S(1)} %shard_map.88), channel_id=1, source_target_pairs={{0,0},{1,9},{2,18},{3,27},{4,4},{5,13},{6,22},{7,31},{8,1},{9,8},{... | collective-permute-start | bytes 393224 | tf_op jit(solution)/shard_map/ppermute | solution.py:276
  (14 other events, 84.9 us)

commit v3 on v2

--- a/solution.py
+++ b/solution.py
@@ -124,7 +124,7 @@
 
 
 def combine_kernel(n, features, squares, d_att, d_att_sib, *refs):
-    parts, (out, root) = refs[:n], refs[n:]
+    parts, (out, first, second, root) = refs[:n], refs[n:]
     rows, width = parts[0].shape
     total = parts[0][...]
     sums = squares[0:1, :]
@@ -135,6 +135,8 @@
     root[...] = scale
     out[:, :width] = (total * scale[:, :1]).astype(BF16)
     out[:, width:] = (d_att[...] + d_att_sib[...]).astype(BF16)
+    first[...] = out[: rows // 2, :]
+    second[...] = out[rows // 2 :, :]
 
 
 def cotangent_kernel(n, *refs):
@@ -157,15 +159,14 @@
     return jnp.where(lane == 0, high, jnp.where(lane == 1, column - high, 0.0)).astype(BF16)
 
 
-def attention_kernel(n, features, mask, *refs):
-    blocks = refs[:n]
-    attended_out, d_proj, held, probs_held, d_scores_held = refs[n:]
+def attention_kernel(n, rows, features, starts, mask, *refs):
+    blocks = refs[: len(starts)]
+    attended_out, d_proj, held, probs_held, d_scores_held = refs[len(starts) :]
     _, _, plane = place()
-    rows = blocks[0].shape[0]
     head = blocks[0].shape[1] // 4
     factor = 1.0 / math.sqrt(head)
-    for e in range(n):
-        held[e * rows : (e + 1) * rows, :] = blocks[e][...]
+    for start, block in zip(starts, blocks):
+        held[start : start + block.shape[0], :] = block[...]
     key = held[:, head : 2 * head]
     value = held[:, 2 * head : 3 * head]
     column_block = lax.broadcasted_iota(jnp.int32, (1, n * rows), 1) // rows
@@ -337,14 +338,24 @@
         scratch=[pltpu.VMEM((n, rows, feats), BF16)],
     )
     d_att_sib = swap(d_att_sib)
-    mixed, root = call(
+    mixed, first, second, root = call(
         functools.partial(combine_kernel, n, features),
-        (shape(rows, width + head), shape(rows, rows, dtype=F32)),
+        (shape(rows, width + head),)
+        + (shape(rows // 2, width + head),) * 2
+        + (shape(rows, rows, dtype=F32),),
         own_squares, d_att, d_att_sib, parts[0], *parts[:0:-1],
     )
-    mixed = [mixed] + [to_plane(mixed, e) for e in range(1, n)]
+    if n == 4:
+        near = [to_plane(first, 1), to_plane(second, 1)]
+        far = [to_plane(first, 2), to_plane(second, 2)]
+        third = [to_plane(first, 3), to_plane(far[1], 1)]
+        mixed = [mixed, *near, *far, *third]
+        starts = [0, rows, 3 * rows // 2, 2 * rows, 5 * rows // 2, 3 * rows, 7 * rows // 2]
+    else:
+        mixed = [mixed] + [to_plane(mixed, e) for e in range(1, n)]
+        starts = [e * rows for e in range(n)]
     attended, d_proj = call(
-        functools.partial(attention_kernel, n, features),
+        functools.partial(attention_kernel, n, rows, features, starts),
         (shape(rows, head + STAT), shape(tokens, width)),
         block_mask, *mixed,
         smem=(0,),

time: 84.1 us -> 82.6 us (0.982)
  waiting for transfers between devices: 35.8 us -> 32.9 us
  starting transfers between devices: 37.6 us -> 39.4 us
    ppermute x32 -> x35, waiting for transfers between devices: 35.8 us -> 32.9 us  [move(): return lax.ppermute(value, AXES, pairs)]
    ppermute x32 -> x35, starting transfers between devices: 37.6 us -> 39.4 us  [move(): return lax.ppermute(value, AXES, pairs)]
  transfers between devices with their start and end apart: 32 -> 35, of which waited for: 16 -> 19; matrix products, arithmetic and copies ran while one was open for 0% -> 0% of each run, Pallas kernels for 6% -> 6%
where the time goes in v3:
time: 82.6 us; the launch traced here: 82.4 us
  starting transfers between devices  39.4 us (48%)
  waiting for transfers between devices  32.9 us (40%)
  Pallas kernels  8.07 us (10%)
  local copies, waits for them, and re-layouts  1.25 us (2%)
  between operations  0.84 us (1%)
    ppermute x35, starting transfers between devices, move(): return lax.ppermute(value, AXES, pairs)  39.4 us
    ppermute x35, waiting for transfers between devices, move(): return lax.ppermute(value, AXES, pairs)  32.9 us
    pallas_call x13, Pallas kernels, call(): pl.pallas_call(kernel, out_shape=out_shape, in_specs=specs, out_specs=jax...  8.07 us
  transfers between devices with their start and end apart: 35, of which 19 were waited for; matrix products, arithmetic and copies ran while one was open for 0% of the time, Pallas kernels for 6%

profile of v3, /device:TPU:24, one launch (start us, length us, event | category | flops | bytes accessed | tf_op | source)
XLA Modules:
  0.0 82.4 jit_solution(54948631449081957)
XLA Ops:
  1.2 4.0 %collective-permute-start = (bf16[128,512]{1,0:T(8,128)(2,1)}, bf16[128,512]{1,0:T(8,128)(2,1)S(1)}, u32[]{:S(2)}, u32[]{:S(2)}) collective-permute-start(bf16[128,512]{1,0:T(8,128)(2,1)} %x.3), channel_id=1, source_target_pairs={{0,0},{1,8},{2,16},{3,24},{4,4},{5,12},{6,20},{7,28},{8,9},{9,1},{... | collective-permute-start | bytes 393224 | tf_op jit(solution)/shard_map/ppermute | solution.py:277
  6.7 2.1 %collective-permute-start.3 = (bf16[128,512]{1,0:T(8,128)(2,1)}, bf16[128,512]{1,0:T(8,128)(2,1)S(1)}, u32[]{:S(2)}, u32[]{:S(2)}) collective-permute-start(bf16[128,512]{1,0:T(8,128)(2,1)} %cot.1), channel_id=1, source_target_pairs={{0,24},{1,25},{2,26},{3,27},{4,28},{5,29},{6,30},{7,31},{8,16},{9,... | collective-permute-start | bytes 393224 | tf_op jit(solution)/shard_map/ppermute | solution.py:277
  10.4 1.2 %collective-permute-done.x = bf16[128,512]{1,0:T(8,128)(2,1)S(1)} collective-permute-done((bf16[128,512]{1,0:T(8,128)(2,1)}, bf16[128,512]{1,0:T(8,128)(2,1)S(1)}, u32[]{:S(2)}, u32[]{:S(2)}) %collective-permute-start) | collective-permute-done | bytes 131104 | tf_op jit(solution)/shard_map/ppermute | solution.py:277
  12.5 4.8 %collective-permute-done.3.refs_3_ = bf16[128,512]{1,0:T(8,128)(2,1)S(1)} collective-permute-done((bf16[128,512]{1,0:T(8,128)(2,1)}, bf16[128,512]{1,0:T(8,128)(2,1)S(1)}, u32[]{:S(2)}, u32[]{:S(2)}) %collective-permute-start.3) | collective-permute-done | bytes 131104 | tf_op jit(solution)/shard_map/ppermute | solution.py:277
  17.4 4.3 %collective-permute-start.8 = (bf16[144,512]{1,0:T(8,128)(2,1)S(1)}, bf16[144,512]{1,0:T(8,128)(2,1)S(1)}, u32[]{:S(2)}, u32[]{:S(2)}) collective-permute-start(bf16[144,512]{1,0:T(8,128)(2,1)S(1)} %shard_map.77.refs_0_), channel_id=1, source_target_pairs={{0,16},{1,17},{2,18},{3,19},{4,20},{5,21},{6,22},{7,23},{8,24},{9,... | collective-permute-start | bytes 442376 | tf_op jit(solution)/shard_map/ppermute | solution.py:277
  21.7 1.4 %collective-permute-start.9 = (bf16[144,512]{1,0:T(8,128)(2,1)S(1)}, bf16[144,512]{1,0:T(8,128)(2,1)S(1)}, u32[]{:S(2)}, u32[]{:S(2)}) collective-permute-start(bf16[144,512]{1,0:T(8,128)(2,1)S(1)} %shard_map.77.refs_0_), channel_id=1, source_target_pairs={{0,24},{1,25},{2,26},{3,27},{4,28},{5,29},{6,30},{7,31},{8,16},{9,... | collective-permute-start | bytes 442376 | tf_op jit(solution)/shard_map/ppermute | solution.py:277
  23.6 1.5 %collective-permute-start.15 = (bf16[256,512]{1,0:T(8,128)(2,1)S(1)}, bf16[256,512]{1,0:T(8,128)(2,1)S(1)}, u32[]{:S(2)}, u32[]{:S(2)}) collective-permute-start(bf16[256,512]{1,0:T(8,128)(2,1)S(1)} %collective-permute-done.7.refs_6_.refs_2_), channel_id=1, source_target_pairs={{0,1},{1,0},{2,3},{3,2},{4,5},{5,4},{6,7},{7,6},{8,9},{9,8},{10,11... | collective-permute-start | bytes 786440 | tf_op jit(solution)/shard_map/ppermute | solution.py:277
  25.1 3.4 %collective-permute-done.8.refs_2_ = bf16[144,512]{1,0:T(8,128)(2,1)S(1)} collective-permute-done((bf16[144,512]{1,0:T(8,128)(2,1)S(1)}, bf16[144,512]{1,0:T(8,128)(2,1)S(1)}, u32[]{:S(2)}, u32[]{:S(2)}) %collective-permute-start.8) | collective-permute-done | bytes 147488 | tf_op jit(solution)/shard_map/ppermute | solution.py:277
  28.5 1.9 %collective-permute-done.9.refs_3_ = bf16[144,512]{1,0:T(8,128)(2,1)S(1)} collective-permute-done((bf16[144,512]{1,0:T(8,128)(2,1)S(1)}, bf16[144,512]{1,0:T(8,128)(2,1)S(1)}, u32[]{:S(2)}, u32[]{:S(2)}) %collective-permute-start.9) | collective-permute-done | bytes 147488 | tf_op jit(solution)/shard_map/ppermute | solution.py:277
  33.9 3.9 %collective-permute-start.19 = (bf16[144,384]{1,0:T(8,128)(2,1)S(1)}, bf16[144,384]{1,0:T(8,128)(2,1)S(1)}, u32[]{:S(2)}, u32[]{:S(2)}) collective-permute-start(bf16[144,384]{1,0:T(8,128)(2,1)S(1)} %get-tuple-element.58), channel_id=1, source_target_pairs={{0,1},{1,0},{2,3},{3,2},{4,5},{5,4},{6,7},{7,6},{8,9},{9,8},{10,11... | collective-permute-start | bytes 331784 | tf_op jit(solution)/shard_map/ppermute | solution.py:277
  38.3 2.8 %collective-permute-done.17.refs_1_ = bf16[144,384]{1,0:T(8,128)(2,1)S(1)} collective-permute-done((bf16[144,384]{1,0:T(8,128)(2,1)S(1)}, bf16[144,384]{1,0:T(8,128)(2,1)S(1)}, u32[]{:S(2)}, u32[]{:S(2)}) %collective-permute-start.17) | collective-permute-done | bytes 110624 | tf_op jit(solution)/shard_map/ppermute | solution.py:277
  41.2 3.1 %collective-permute-done.18.refs_2_ = bf16[144,384]{1,0:T(8,128)(2,1)S(1)} collective-permute-done((bf16[144,384]{1,0:T(8,128)(2,1)S(1)}, bf16[144,384]{1,0:T(8,128)(2,1)S(1)}, u32[]{:S(2)}, u32[]{:S(2)}) %collective-permute-start.18) | collective-permute-done | bytes 110624 | tf_op jit(solution)/shard_map/ppermute | solution.py:277
  44.5 1.4 %collective-permute-start.23 = (bf16[64,512]{1,0:T(8,128)(2,1)S(1)}, bf16[64,512]{1,0:T(8,128)(2,1)S(1)}, u32[]{:S(2)}, u32[]{:S(2)}) collective-permute-start(bf16[64,512]{1,0:T(8,128)(2,1)S(1)} %get-tuple-element.61), channel_id=1, source_target_pairs={{0,2},{1,3},{2,0},{3,1},{4,6},{5,7},{6,4},{7,5},{8,10},{9,11},{10,... | collective-permute-start | bytes 196616 | tf_op jit(solution)/shard_map/ppermute | solution.py:277
  48.0 1.6 %collective-permute-start.22 = (bf16[64,512]{1,0:T(8,128)(2,1)S(1)}, bf16[64,512]{1,0:T(8,128)(2,1)S(1)}, u32[]{:S(2)}, u32[]{:S(2)}) collective-permute-start(bf16[64,512]{1,0:T(8,128)(2,1)S(1)} %get-tuple-element.60), channel_id=1, source_target_pairs={{0,2},{1,3},{2,0},{3,1},{4,6},{5,7},{6,4},{7,5},{8,10},{9,11},{10,... | collective-permute-start | bytes 196616 | tf_op jit(solution)/shard_map/ppermute | solution.py:277
  49.5 1.9 %collective-permute-start.24 = (bf16[64,512]{1,0:T(8,128)(2,1)S(1)}, bf16[64,512]{1,0:T(8,128)(2,1)S(1)}, u32[]{:S(2)}, u32[]{:S(2)}) collective-permute-start(bf16[64,512]{1,0:T(8,128)(2,1)S(1)} %get-tuple-element.60), channel_id=1, source_target_pairs={{0,3},{1,2},{2,1},{3,0},{4,7},{5,6},{6,5},{7,4},{8,11},{9,10},{10,... | collective-permute-start | bytes 196616 | tf_op jit(solution)/shard_map/ppermute | solution.py:277
  51.5 2.4 %collective-permute-done.20.refs_1_ = bf16[64,512]{1,0:T(8,128)(2,1)S(1)} collective-permute-done((bf16[64,512]{1,0:T(8,128)(2,1)S(1)}, bf16[64,512]{1,0:T(8,128)(2,1)S(1)}, u32[]{:S(2)}, u32[]{:S(2)}) %collective-permute-start.20) | collective-permute-done | bytes 65568 | tf_op jit(solution)/shard_map/ppermute | solution.py:277
  56.3 2.0 %shard_map.83 = (bf16[128,256]{1,0:T(8,128)(2,1)S(1)}, bf16[512,384]{1,0:T(8,128)(2,1)S(1)}) custom-call(s32[4,4]{1,0:T(4,128)S(1)} %copy-done.4, bf16[128,512]{1,0:T(8,128)(2,1)S(1)} %get-tuple-element.59.refs_0_, bf16[64,512]{1,0:T(8,128)(2,1)S(1)} %collective-permute-done.20.refs_1_, bf16[64,512]{1,0:T(8,128)(2,1)S(1)} %collective-permute-done.21.refs_2_, ...), custom_call_target="tpu_custom_call" | custom-call | tf_op jit(solution)/shard_map/pallas_call | solution.py:46
  61.7 1.4 %collective-permute-start.32 = (bf16[128,512]{1,0:T(8,128)(2,1)S(1)}, bf16[128,512]{1,0:T(8,128)(2,1)S(1)}, u32[]{:S(2)}, u32[]{:S(2)}) collective-permute-start(bf16[128,512]{1,0:T(8,128)(2,1)S(1)} %get-tuple-element.76), channel_id=1, source_target_pairs={{0,16},{1,17},{2,18},{3,19},{4,20},{5,21},{6,22},{7,23},{8,24},{9,... | collective-permute-start | bytes 393224 | tf_op jit(solution)/shard_map/ppermute | solution.py:277
  65.8 1.4 %collective-permute-start.29 = (bf16[144,512]{1,0:T(8,128)(2,1)S(1)}, bf16[144,512]{1,0:T(8,128)(2,1)S(1)}, u32[]{:S(2)}, u32[]{:S(2)}) collective-permute-start(bf16[144,512]{1,0:T(8,128)(2,1)S(1)} %get-tuple-element.67), channel_id=1, source_target_pairs={{0,16},{1,17},{2,18},{3,19},{4,20},{5,21},{6,22},{7,23},{8,24},{9,... | collective-permute-start | bytes 442376 | tf_op jit(solution)/shard_map/ppermute | solution.py:277
  67.1 1.5 %collective-permute-start.30 = (bf16[144,512]{1,0:T(8,128)(2,1)S(1)}, bf16[144,512]{1,0:T(8,128)(2,1)S(1)}, u32[]{:S(2)}, u32[]{:S(2)}) collective-permute-start(bf16[144,512]{1,0:T(8,128)(2,1)S(1)} %get-tuple-element.68), channel_id=1, source_target_pairs={{0,24},{1,25},{2,26},{3,27},{4,28},{5,29},{6,30},{7,31},{8,16},{9,... | collective-permute-start | bytes 442376 | tf_op jit(solution)/shard_map/ppermute | solution.py:277
  68.8 2.2 %collective-permute-done.33.refs_3_ = bf16[128,512]{1,0:T(8,128)(2,1)S(1)} collective-permute-done((bf16[128,512]{1,0:T(8,128)(2,1)S(1)}, bf16[128,512]{1,0:T(8,128)(2,1)S(1)}, u32[]{:S(2)}, u32[]{:S(2)}) %collective-permute-start.33) | collective-permute-done | bytes 131104 | tf_op jit(solution)/shard_map/ppermute | solution.py:277
  71.1 3.6 %collective-permute-start.34 = (bf16[128,512]{1,0:T(8,128)(2,1)S(1)}, bf16[128,512]{1,0:T(8,128)(2,1)S(1)}, u32[]{:S(2)}, u32[]{:S(2)}) collective-permute-start(bf16[128,512]{1,0:T(8,128)(2,1)S(1)} %shard_map.88), channel_id=1, source_target_pairs={{0,0},{1,9},{2,18},{3,27},{4,4},{5,13},{6,22},{7,31},{8,1},{9,8},{... | collective-permute-start | bytes 393224 | tf_op jit(solution)/shard_map/ppermute | solution.py:277
  74.7 1.8 %collective-permute-done.29.refs_2_ = bf16[144,512]{1,0:T(8,128)(2,1)S(1)} collective-permute-done((bf16[144,512]{1,0:T(8,128)(2,1)S(1)}, bf16[144,512]{1,0:T(8,128)(2,1)S(1)}, u32[]{:S(2)}, u32[]{:S(2)}) %collective-permute-start.29) | collective-permute-done | bytes 147488 | tf_op jit(solution)/shard_map/ppermute | solution.py:277
  77.3 4.3 %collective-permute-done.34.grad = bf16[128,512]{1,0:T(8,128)(2,1)S(1)} collective-permute-done((bf16[128,512]{1,0:T(8,128)(2,1)S(1)}, bf16[128,512]{1,0:T(8,128)(2,1)S(1)}, u32[]{:S(2)}, u32[]{:S(2)}) %collective-permute-start.34) | collective-permute-done | bytes 131104 | tf_op jit(solution)/shard_map/ppermute | solution.py:277
  (72 shorter events, 21.9 us)
Async XLA Ops:
  0.6 8.1 %collective-permute-start.6 = (bf16[1024,384]{1,0:T(8,128)(2,1)}, bf16[1024,384]{1,0:T(8,128)(2,1)S(1)}, u32[]{:S(2)}, u32[]{:S(2)}) collective-permute-start(bf16[1024,384]{1,0:T(8,128)(2,1)} %bitcast.2), channel_id=1, source_target_pairs={{0,4},{1,5},{2,6},{3,7},{4,0},{5,1},{6,2},{7,3},{8,12},{9,13},{10,... | collective-permute-start | bytes 2359304 | tf_op jit(solution)/shard_map/ppermute | solution.py:277
  1.2 10.4 %collective-permute-start = (bf16[128,512]{1,0:T(8,128)(2,1)}, bf16[128,512]{1,0:T(8,128)(2,1)S(1)}, u32[]{:S(2)}, u32[]{:S(2)}) collective-permute-start(bf16[128,512]{1,0:T(8,128)(2,1)} %x.3), channel_id=1, source_target_pairs={{0,0},{1,8},{2,16},{3,24},{4,4},{5,12},{6,20},{7,28},{8,9},{9,1},{... | collective-permute-start | bytes 393224 | tf_op jit(solution)/shard_map/ppermute | solution.py:277
  5.2 6.7 %collective-permute-start.1 = (bf16[128,512]{1,0:T(8,128)(2,1)}, bf16[128,512]{1,0:T(8,128)(2,1)S(1)}, u32[]{:S(2)}, u32[]{:S(2)}) collective-permute-start(bf16[128,512]{1,0:T(8,128)(2,1)} %cot.1), channel_id=1, source_target_pairs={{0,8},{1,9},{2,10},{3,11},{4,12},{5,13},{6,14},{7,15},{8,0},{9,1},... | collective-permute-start | bytes 393224 | tf_op jit(solution)/shard_map/ppermute | solution.py:277
  5.9 6.6 %collective-permute-start.2 = (bf16[128,512]{1,0:T(8,128)(2,1)}, bf16[128,512]{1,0:T(8,128)(2,1)S(1)}, u32[]{:S(2)}, u32[]{:S(2)}) collective-permute-start(bf16[128,512]{1,0:T(8,128)(2,1)} %cot.1), channel_id=1, source_target_pairs={{0,16},{1,17},{2,18},{3,19},{4,20},{5,21},{6,22},{7,23},{8,24},{9,... | collective-permute-start | bytes 393224 | tf_op jit(solution)/shard_map/ppermute | solution.py:277
  6.7 10.6 %collective-permute-start.3 = (bf16[128,512]{1,0:T(8,128)(2,1)}, bf16[128,512]{1,0:T(8,128)(2,1)S(1)}, u32[]{:S(2)}, u32[]{:S(2)}) collective-permute-start(bf16[128,512]{1,0:T(8,128)(2,1)} %cot.1), channel_id=1, source_target_pairs={{0,24},{1,25},{2,26},{3,27},{4,28},{5,29},{6,30},{7,31},{8,16},{9,... | collective-permute-start | bytes 393224 | tf_op jit(solution)/shard_map/ppermute | solution.py:277
  9.8 13.9 %collective-permute-start.7 = (bf16[256,512]{1,0:T(8,128)(2,1)S(1)}, bf16[256,512]{1,0:T(8,128)(2,1)S(1)}, u32[]{:S(2)}, u32[]{:S(2)}) collective-permute-start(bf16[256,512]{1,0:T(8,128)(2,1)S(1)} %shard_map.78.refs_4_.refs_0_), channel_id=1, source_target_pairs={{0,2},{1,3},{2,0},{3,1},{4,6},{5,7},{6,4},{7,5},{8,10},{9,11},{10,... | collective-permute-start | bytes 786440 | tf_op jit(solution)/shard_map/ppermute | solution.py:277
  17.4 11.1 %collective-permute-start.8 = (bf16[144,512]{1,0:T(8,128)(2,1)S(1)}, bf16[144,512]{1,0:T(8,128)(2,1)S(1)}, u32[]{:S(2)}, u32[]{:S(2)}) collective-permute-start(bf16[144,512]{1,0:T(8,128)(2,1)S(1)} %shard_map.77.refs_0_), channel_id=1, source_target_pairs={{0,16},{1,17},{2,18},{3,19},{4,20},{5,21},{6,22},{7,23},{8,24},{9,... | collective-permute-start | bytes 442376 | tf_op jit(solution)/shard_map/ppermute | solution.py:277
  21.7 8.7 %collective-permute-start.9 = (bf16[144,512]{1,0:T(8,128)(2,1)S(1)}, bf16[144,512]{1,0:T(8,128)(2,1)S(1)}, u32[]{:S(2)}, u32[]{:S(2)}) collective-permute-start(bf16[144,512]{1,0:T(8,128)(2,1)S(1)} %shard_map.77.refs_0_), channel_id=1, source_target_pairs={{0,24},{1,25},{2,26},{3,27},{4,28},{5,29},{6,30},{7,31},{8,16},{9,... | collective-permute-start | bytes 442376 | tf_op jit(solution)/shard_map/ppermute | solution.py:277
  23.1 14.7 %collective-permute-start.14 = (bf16[256,512]{1,0:T(8,128)(2,1)S(1)}, bf16[256,512]{1,0:T(8,128)(2,1)S(1)}, u32[]{:S(2)}, u32[]{:S(2)}) collective-permute-start(bf16[256,512]{1,0:T(8,128)(2,1)S(1)} %shard_map.78.refs_4_.refs_0_), channel_id=1, source_target_pairs={{0,1},{1,0},{2,3},{3,2},{4,5},{5,4},{6,7},{7,6},{8,9},{9,8},{10,11... | collective-permute-start | bytes 786440 | tf_op jit(solution)/shard_map/ppermute | solution.py:277
  23.6 14.2 %collective-permute-start.15 = (bf16[256,512]{1,0:T(8,128)(2,1)S(1)}, bf16[256,512]{1,0:T(8,128)(2,1)S(1)}, u32[]{:S(2)}, u32[]{:S(2)}) collective-permute-start(bf16[256,512]{1,0:T(8,128)(2,1)S(1)} %collective-permute-done.7.refs_6_.refs_2_), channel_id=1, source_target_pairs={{0,1},{1,0},{2,3},{3,2},{4,5},{5,4},{6,7},{7,6},{8,9},{9,8},{10,11... | collective-permute-start | bytes 786440 | tf_op jit(solution)/shard_map/ppermute | solution.py:277
  33.3 7.9 %collective-permute-start.17 = (bf16[144,384]{1,0:T(8,128)(2,1)S(1)}, bf16[144,384]{1,0:T(8,128)(2,1)S(1)}, u32[]{:S(2)}, u32[]{:S(2)}) collective-permute-start(bf16[144,384]{1,0:T(8,128)(2,1)S(1)} %get-tuple-element.56), channel_id=1, source_target_pairs={{0,3},{1,2},{2,1},{3,0},{4,7},{5,6},{6,5},{7,4},{8,11},{9,10},{10,... | collective-permute-start | bytes 331784 | tf_op jit(solution)/shard_map/ppermute | solution.py:277
  33.4 10.9 %collective-permute-start.18 = (bf16[144,384]{1,0:T(8,128)(2,1)S(1)}, bf16[144,384]{1,0:T(8,128)(2,1)S(1)}, u32[]{:S(2)}, u32[]{:S(2)}) collective-permute-start(bf16[144,384]{1,0:T(8,128)(2,1)S(1)} %get-tuple-element.57), channel_id=1, source_target_pairs={{0,2},{1,3},{2,0},{3,1},{4,6},{5,7},{6,4},{7,5},{8,10},{9,11},{10,... | collective-permute-start | bytes 331784 | tf_op jit(solution)/shard_map/ppermute | solution.py:277
  33.9 10.4 %collective-permute-start.19 = (bf16[144,384]{1,0:T(8,128)(2,1)S(1)}, bf16[144,384]{1,0:T(8,128)(2,1)S(1)}, u32[]{:S(2)}, u32[]{:S(2)}) collective-permute-start(bf16[144,384]{1,0:T(8,128)(2,1)S(1)} %get-tuple-element.58), channel_id=1, source_target_pairs={{0,1},{1,0},{2,3},{3,2},{4,5},{5,4},{6,7},{7,6},{8,9},{9,8},{10,11... | collective-permute-start | bytes 331784 | tf_op jit(solution)/shard_map/ppermute | solution.py:277
  44.5 7.0 %collective-permute-start.23 = (bf16[64,512]{1,0:T(8,128)(2,1)S(1)}, bf16[64,512]{1,0:T(8,128)(2,1)S(1)}, u32[]{:S(2)}, u32[]{:S(2)}) collective-permute-start(bf16[64,512]{1,0:T(8,128)(2,1)S(1)} %get-tuple-element.61), channel_id=1, source_target_pairs={{0,2},{1,3},{2,0},{3,1},{4,6},{5,7},{6,4},{7,5},{8,10},{9,11},{10,... | collective-permute-start | bytes 196616 | tf_op jit(solution)/shard_map/ppermute | solution.py:277
  45.9 7.9 %collective-permute-start.21 = (bf16[64,512]{1,0:T(8,128)(2,1)S(1)}, bf16[64,512]{1,0:T(8,128)(2,1)S(1)}, u32[]{:S(2)}, u32[]{:S(2)}) collective-permute-start(bf16[64,512]{1,0:T(8,128)(2,1)S(1)} %get-tuple-element.61), channel_id=1, source_target_pairs={{0,1},{1,0},{2,3},{3,2},{4,5},{5,4},{6,7},{7,6},{8,9},{9,8},{10,11... | collective-permute-start | bytes 196616 | tf_op jit(solution)/shard_map/ppermute | solution.py:277
  47.1 6.8 %collective-permute-start.20 = (bf16[64,512]{1,0:T(8,128)(2,1)S(1)}, bf16[64,512]{1,0:T(8,128)(2,1)S(1)}, u32[]{:S(2)}, u32[]{:S(2)}) collective-permute-start(bf16[64,512]{1,0:T(8,128)(2,1)S(1)} %get-tuple-element.60), channel_id=1, source_target_pairs={{0,1},{1,0},{2,3},{3,2},{4,5},{5,4},{6,7},{7,6},{8,9},{9,8},{10,11... | collective-permute-start | bytes 196616 | tf_op jit(solution)/shard_map/ppermute | solution.py:277
  48.0 6.7 %collective-permute-start.22 = (bf16[64,512]{1,0:T(8,128)(2,1)S(1)}, bf16[64,512]{1,0:T(8,128)(2,1)S(1)}, u32[]{:S(2)}, u32[]{:S(2)}) collective-permute-start(bf16[64,512]{1,0:T(8,128)(2,1)S(1)} %get-tuple-element.60), channel_id=1, source_target_pairs={{0,2},{1,3},{2,0},{3,1},{4,6},{5,7},{6,4},{7,5},{8,10},{9,11},{10,... | collective-permute-start | bytes 196616 | tf_op jit(solution)/shard_map/ppermute | solution.py:277
  60.7 6.4 %collective-permute-start.31 = (bf16[128,512]{1,0:T(8,128)(2,1)S(1)}, bf16[128,512]{1,0:T(8,128)(2,1)S(1)}, u32[]{:S(2)}, u32[]{:S(2)}) collective-permute-start(bf16[128,512]{1,0:T(8,128)(2,1)S(1)} %get-tuple-element.75), channel_id=1, source_target_pairs={{0,8},{1,9},{2,10},{3,11},{4,12},{5,13},{6,14},{7,15},{8,0},{9,1},... | collective-permute-start | bytes 393224 | tf_op jit(solution)/shard_map/ppermute | solution.py:277
  61.7 7.0 %collective-permute-start.32 = (bf16[128,512]{1,0:T(8,128)(2,1)S(1)}, bf16[128,512]{1,0:T(8,128)(2,1)S(1)}, u32[]{:S(2)}, u32[]{:S(2)}) collective-permute-start(bf16[128,512]{1,0:T(8,128)(2,1)S(1)} %get-tuple-element.76), channel_id=1, source_target_pairs={{0,16},{1,17},{2,18},{3,19},{4,20},{5,21},{6,22},{7,23},{8,24},{9,... | collective-permute-start | bytes 393224 | tf_op jit(solution)/shard_map/ppermute | solution.py:277
  63.1 7.9 %collective-permute-start.33 = (bf16[128,512]{1,0:T(8,128)(2,1)S(1)}, bf16[128,512]{1,0:T(8,128)(2,1)S(1)}, u32[]{:S(2)}, u32[]{:S(2)}) collective-permute-start(bf16[128,512]{1,0:T(8,128)(2,1)S(1)} %get-tuple-element.77), channel_id=1, source_target_pairs={{0,24},{1,25},{2,26},{3,27},{4,28},{5,29},{6,30},{7,31},{8,16},{9,... | collective-permute-start | bytes 393224 | tf_op jit(solution)/shard_map/ppermute | solution.py:277
  64.7 9.9 %collective-permute-start.28 = (bf16[144,512]{1,0:T(8,128)(2,1)S(1)}, bf16[144,512]{1,0:T(8,128)(2,1)S(1)}, u32[]{:S(2)}, u32[]{:S(2)}) collective-permute-start(bf16[144,512]{1,0:T(8,128)(2,1)S(1)} %get-tuple-element.66), channel_id=1, source_target_pairs={{0,8},{1,9},{2,10},{3,11},{4,12},{5,13},{6,14},{7,15},{8,0},{9,1},... | collective-permute-start | bytes 442376 | tf_op jit(solution)/shard_map/ppermute | solution.py:277
  65.8 10.7 %collective-permute-start.29 = (bf16[144,512]{1,0:T(8,128)(2,1)S(1)}, bf16[144,512]{1,0:T(8,128)(2,1)S(1)}, u32[]{:S(2)}, u32[]{:S(2)}) collective-permute-start(bf16[144,512]{1,0:T(8,128)(2,1)S(1)} %get-tuple-element.67), channel_id=1, source_target_pairs={{0,16},{1,17},{2,18},{3,19},{4,20},{5,21},{6,22},{7,23},{8,24},{9,... | collective-permute-start | bytes 442376 | tf_op jit(solution)/shard_map/ppermute | solution.py:277
  67.1 9.4 %collective-permute-start.30 = (bf16[144,512]{1,0:T(8,128)(2,1)S(1)}, bf16[144,512]{1,0:T(8,128)(2,1)S(1)}, u32[]{:S(2)}, u32[]{:S(2)}) collective-permute-start(bf16[144,512]{1,0:T(8,128)(2,1)S(1)} %get-tuple-element.68), channel_id=1, source_target_pairs={{0,24},{1,25},{2,26},{3,27},{4,28},{5,29},{6,30},{7,31},{8,16},{9,... | collective-permute-start | bytes 442376 | tf_op jit(solution)/shard_map/ppermute | solution.py:277
  71.1 10.6 %collective-permute-start.34 = (bf16[128,512]{1,0:T(8,128)(2,1)S(1)}, bf16[128,512]{1,0:T(8,128)(2,1)S(1)}, u32[]{:S(2)}, u32[]{:S(2)}) collective-permute-start(bf16[128,512]{1,0:T(8,128)(2,1)S(1)} %shard_map.88), channel_id=1, source_target_pairs={{0,0},{1,9},{2,18},{3,27},{4,4},{5,13},{6,22},{7,31},{8,1},{9,8},{... | collective-permute-start | bytes 393224 | tf_op jit(solution)/shard_map/ppermute | solution.py:277
  (17 other events, 100.7 us)
